TPU v7x, 256 devices: a whole 4x4x8 slice. The times are simulated.
256 devices in a mesh: seq: 32 (over x, z_lo, core), chan: 8 (over y, z_hi).
Axes of the slice: x: 4, y: 4, z: 8 (z_hi: 2, z_lo: 4; z = z_hi * 4 + z_lo), core: 2. Of those that a mesh axis runs over, the one named last changes fastest.
Arguments:
- gate_act: bfloat16 [1920, 16384], P('chan', 'seq'), may hold values from -3 to 3
- key_act: bfloat16 [1920, 16384], P('chan', 'seq'), may hold values from -6 to 6
- value_act: bfloat16 [1920, 16384], P('chan', 'seq'), may hold values from -6 to 6
- filter_raw: float32 [1920, 16384], P('chan', 'seq'), may hold values from -6 to 6
- decay_rate: float32 [1920], P('chan'), as said below
- out_weight: bfloat16 [1920, 1920], P('chan'), may hold values from -0.125 to 0.125
- out_grad: bfloat16 [1920, 16384], P('chan', 'seq'), may hold values from -6 to 6
Outputs:
- gate_grad: bfloat16 [1920, 16384], P('chan', 'seq')
- key_grad: bfloat16 [1920, 16384], P('chan', 'seq')
- value_grad: bfloat16 [1920, 16384], P('chan', 'seq')
- filter_grad: float32 [1920, 16384], P('chan', 'seq')
- weight_grad: float32 [1920, 1920], P('chan', 'seq')
Inputs may be any that keep to these rules, and one draw needn't show every extreme that they name: `decay_rate`: rates are positive and at most 1/30 per position.
All inputs are finite; a program needn't handle non-finite values.
Results may differ from a plain program's by a relative error of at most 0.0045.
Values may be sent and summed in bfloat16 or wider, within the bound.
A program may use at most 128 MiB of HBM per device.

v0:
```python
import math

import jax
import jax.numpy as jnp
from jax import lax
from jax.sharding import PartitionSpec as P

precise = lax.Precision.HIGHEST


def iota_grid(layout, axis_number):
    return lax.broadcasted_iota(jnp.int32, layout, axis_number)


def spectral_bin(owner, member, pieces):
    return jnp.where(member == 0, owner, jnp.where(owner == 0, pieces, 2 * pieces - owner))


def phase_table(exponent, period, direction):
    residue = exponent % period
    quarter = (8 * residue + period) // (2 * period)
    offset = 4 * residue - quarter * period
    small = offset.astype(jnp.float32) * (math.pi / (2.0 * period))
    cos_small = jnp.cos(small)
    sin_small = jnp.sin(small)
    turn = quarter % 4
    cosine = jnp.where(
        turn == 0,
        cos_small,
        jnp.where(turn == 1, -sin_small, jnp.where(turn == 2, -cos_small, sin_small)),
    )
    sine_part = jnp.where(
        turn == 0,
        sin_small,
        jnp.where(turn == 1, cos_small, jnp.where(turn == 2, -sin_small, -cos_small)),
    )
    return (cosine, direction * sine_part)


def apply_table(form, phases, signal_pair):
    cosine, sine_part = phases
    real_part = jnp.einsum(form, cosine, signal_pair[0], precision=precise) - jnp.einsum(
        form, sine_part, signal_pair[1], precision=precise
    )
    imag_part = jnp.einsum(form, cosine, signal_pair[1], precision=precise) + jnp.einsum(
        form, sine_part, signal_pair[0], precision=precise
    )
    return jnp.stack([real_part, imag_part])


def rotate(signal_pair, phases):
    cosine, sine_part = phases
    return jnp.stack(
        [
            signal_pair[0] * cosine - signal_pair[1] * sine_part,
            signal_pair[0] * sine_part + signal_pair[1] * cosine,
        ]
    )


def local_transform(signal_pair, direction):
    fields = signal_pair.shape[1]
    pairs = signal_pair.shape[2]
    channels = signal_pair.shape[3]
    length = signal_pair.shape[4]
    leading = math.gcd(length, 2 ** (length.bit_length() // 2))
    second = length // leading
    folded = signal_pair.reshape(2, fields, pairs, channels, second, leading)
    coarse = phase_table(
        iota_grid((second, second), 0) * iota_grid((second, second), 1), second, direction
    )
    sectioned = apply_table("jm,fpcmn->fpcjn", coarse, folded)
    twist_cos, twist_sin = phase_table(
        iota_grid((second, leading), 0) * iota_grid((second, leading), 1), length, direction
    )
    sectioned = rotate(sectioned, (twist_cos, twist_sin))
    finer = phase_table(
        iota_grid((leading, leading), 0) * iota_grid((leading, leading), 1), leading, direction
    )
    result = apply_table("kn,fpcjn->fpckj", finer, sectioned)
    return result.reshape(2, fields, pairs, channels, length)


def exchange_tokens(token_rows):
    return lax.all_to_all(token_rows, "seq", split_axis=2, concat_axis=2, tiled=True)


def exchange_frequencies(spectral_rows):
    return lax.all_to_all(spectral_rows, "seq", split_axis=4, concat_axis=4, tiled=True)


def forward_transform(signals):
    fields, channels, length = signals.shape
    pieces = lax.axis_size("seq")
    block_rows = length // pieces
    device_index = lax.axis_index("seq")
    period = 2 * pieces * length
    arrived = exchange_tokens(signals).reshape(fields, channels, pieces, block_rows)
    layout = (2, pieces, pieces)
    cosine, sine_part = phase_table(
        iota_grid(layout, 2) * spectral_bin(iota_grid(layout, 1), iota_grid(layout, 0), pieces),
        2 * pieces,
        -1.0,
    )
    spectral = jnp.stack(
        [
            jnp.einsum("ejb,fcba->fecja", cosine, arrived, precision=precise),
            jnp.einsum("ejb,fcba->fecja", sine_part, arrived, precision=precise),
        ]
    ).reshape(2, fields, 2, channels, length)
    twist_layout = (2, pieces, block_rows)
    exponent = (device_index * block_rows + iota_grid(twist_layout, 2)) * spectral_bin(
        iota_grid(twist_layout, 1), iota_grid(twist_layout, 0), pieces
    )
    twist_cos, twist_sin = phase_table(exponent.reshape(2, length), period, -1.0)
    spectral = rotate(spectral, (twist_cos[:, None, :], twist_sin[:, None, :]))
    spread = exchange_frequencies(spectral)
    result = local_transform(spread, -1.0)
    return result


def inverse_transform(spectra):
    fields = spectra.shape[1]
    channels = spectra.shape[3]
    length = spectra.shape[4]
    pieces = lax.axis_size("seq")
    block_rows = length // pieces
    device_index = lax.axis_index("seq")
    period = 2 * pieces * length
    signal_pair = local_transform(spectra, 1.0)
    twist_layout = (2, length)
    exponent = iota_grid(twist_layout, 1) * spectral_bin(
        device_index, iota_grid(twist_layout, 0), pieces
    )
    twist_cos, twist_sin = phase_table(exponent, period, 1.0)
    signal_pair = rotate(signal_pair, (twist_cos[:, None, :], twist_sin[:, None, :]))
    spread = exchange_frequencies(signal_pair).reshape(2, fields, 2, channels, pieces, block_rows)
    layout = (pieces, 2, pieces)
    cosine, sine_part = phase_table(
        iota_grid(layout, 0) * spectral_bin(iota_grid(layout, 2), iota_grid(layout, 1), pieces),
        2 * pieces,
        1.0,
    )
    cosine = cosine * (1.0 / period)
    sine_part = sine_part * (1.0 / period)
    real_part = jnp.einsum("bej,fecja->fcba", cosine, spread[0], precision=precise) - jnp.einsum(
        "bej,fecja->fcba", sine_part, spread[1], precision=precise
    )
    token_rows = real_part
    token_rows = token_rows.reshape(token_rows.shape[0], channels, length)
    return exchange_tokens(token_rows)


def per_device(gate_act, key_act, value_act, filter_raw, decay_rate, out_weight, out_grad):
    channels, length = gate_act.shape
    device_index = lax.axis_index("seq")
    position = (device_index * length + lax.iota(jnp.int32, length)).astype(jnp.float32)
    envelope = jnp.sqrt(1.0 - jnp.exp(-2.0 * decay_rate))[:, None] * jnp.exp(
        -decay_rate[:, None] * position[None, :]
    )
    kernel = filter_raw * envelope
    gate_full = gate_act.astype(jnp.float32)
    key_full = key_act.astype(jnp.float32)
    value_full = value_act.astype(jnp.float32)
    signal = key_full * value_full
    spectra = forward_transform(jnp.stack([kernel, signal]))
    kernel_spec = spectra[:, 0]
    signal_spec = spectra[:, 1]
    conv_spec = jnp.stack(
        [
            kernel_spec[0] * signal_spec[0] - kernel_spec[1] * signal_spec[1],
            kernel_spec[0] * signal_spec[1] + kernel_spec[1] * signal_spec[0],
        ]
    )
    conv = inverse_transform(conv_spec[:, None])[0]
    gated = (gate_full * conv).astype(jnp.bfloat16)
    shard_part = lax.all_gather(out_grad, "chan", axis=0, tiled=True)
    upstream_sum = jnp.dot(out_weight, shard_part, preferred_element_type=jnp.float32)
    product = lax.dot_general(
        gated, shard_part, (((1,), (1,)), ((), ())), preferred_element_type=jnp.float32
    )
    partial_value = product
    upstream, partial_value = (upstream_sum, partial_value)
    gate_grad = (upstream * conv).astype(jnp.bfloat16)
    conv_grad = upstream * gate_full
    summed = lax.psum(partial_value, "seq")
    columns = partial_value.shape[1] // lax.axis_size("seq")
    weight_grad = lax.dynamic_slice_in_dim(summed, device_index * columns, columns, 1)
    grad_spec = forward_transform(conv_grad[None])[:, 0]
    kernel_back_re = kernel_spec[0] * grad_spec[0] + kernel_spec[1] * grad_spec[1]
    kernel_back_im = kernel_spec[0] * grad_spec[1] - kernel_spec[1] * grad_spec[0]
    signal_back_re = signal_spec[0] * grad_spec[0] + signal_spec[1] * grad_spec[1]
    signal_back_im = signal_spec[0] * grad_spec[1] - signal_spec[1] * grad_spec[0]
    both_specs = jnp.stack(
        [jnp.stack([kernel_back_re, signal_back_re]), jnp.stack([kernel_back_im, signal_back_im])]
    )
    result = inverse_transform(both_specs)
    signal_grad = result[0]
    kernel_grad = result[1]
    key_grad = (signal_grad * value_full).astype(jnp.bfloat16)
    value_grad = (signal_grad * key_full).astype(jnp.bfloat16)
    filter_grad = kernel_grad * envelope
    return (gate_grad, key_grad, value_grad, filter_grad, weight_grad)


def solution(mesh):
    placed = (
        P("chan", "seq"),
        P("chan", "seq"),
        P("chan", "seq"),
        P("chan", "seq"),
        P("chan"),
        P("chan", None),
        P("chan", "seq"),
    )
    return jax.shard_map(
        per_device,
        mesh=mesh,
        in_specs=placed,
        out_specs=(
            P("chan", "seq"),
            P("chan", "seq"),
            P("chan", "seq"),
            P("chan", "seq"),
            P("chan", "seq"),
        ),
        check_vma=False,
    )
```

profile of v0, /device:TPU:16, one launch (start us, length us, event | category | flops | bytes accessed | tf_op | source)
XLA Modules:
  0.0 769.7 jit_solution(11050110924517642625)
XLA Ops:
  10.9 8.8 %all-to-all-start = ((f32[2,240,512]{1,0,2:T(2,128)}), f32[2,240,512]{1,0,2:T(2,128)S(1)}, u32[]{:S(2)}, u32[]{:S(2)}) async-start(f32[2,240,512]{1,0,2:T(2,128)} %copy.196), calls=%async_computation | async-start | bytes 2097152 | tf_op jit(solution)/shard_map/all_to_all | solution.py:85
  20.5 27.1 %all-to-all-done = f32[2,240,512]{1,0,2:T(2,128)S(1)} async-done(((f32[2,240,512]{1,0,2:T(2,128)}), f32[2,240,512]{1,0,2:T(2,128)S(1)}, u32[]{:S(2)}, u32[]{:S(2)}) %all-to-all-start) | async-done | bytes 983072 | tf_op jit(solution)/shard_map/all_to_all | solution.py:85
  47.7 2.7 convolution_bitcast_fusion
  50.4 2.7 convolution_bitcast_fusion.1
  56.4 5.4 copy.202
  61.9 4.9 all-to-all-start.1
  67.1 95.0 %all-to-all-done.1 = f32[2,2,2,240,512]{3,2,1,0,4:T(2,128)} async-done(((f32[2,2,2,240,512]{3,2,1,0,4:T(2,128)}), f32[2,2,2,240,512]{3,2,1,0,4:T(2,128)}, u32[]{:S(2)}, u32[]{:S(2)}) %all-to-all-start.1) | async-done | bytes 3932192 | tf_op jit(solution)/shard_map/all_to_all | solution.py:89
  162.1 3.7 fusion.730
  166.2 3.1 fusion.28
  169.3 3.1 fusion.30
  172.8 3.5 fusion.42
  176.4 3.8 fusion.4
  180.2 3.3 fusion.20
  183.5 3.3 fusion.22
  186.8 3.6 subtract_bitcast_fusion.1
  190.4 3.3 add_bitcast_fusion.1
  196.2 2.2 multiply_subtract_fusion.2
  201.7 2.0 fusion.68
  203.7 1.9 subtract_bitcast_fusion.3
  207.4 1.7 fusion.98
  214.4 3.1 copy.225
  217.5 4.0 all-to-all-start.2
  222.3 76.0 %all-to-all-done.2 = f32[2,1,2,240,512]{3,2,1,0,4:T(2,128)S(1)} async-done(((f32[2,1,2,240,512]{3,2,1,0,4:T(2,128)}), f32[2,1,2,240,512]{3,2,1,0,4:T(2,128)S(1)}, u32[]{:S(2)}, u32[]{:S(2)}) %all-to-all-start.2) | async-done | bytes 1966112 | tf_op jit(solution)/shard_map/all_to_all | solution.py:89
  303.1 20.4 %all_to_all.40 = f32[1,240,512]{1,0,2:T(1,128)S(1)} all-to-all(f32[1,240,512]{1,0,2:T(1,128)S(1)} %copy.231), channel_id=1, replica_groups=mesh['seq'=32,'chan'=8] {'seq'}, dimensions={2} | all-to-all | bytes 983040 | tf_op jit(solution)/shard_map/all_to_all | solution.py:85
  323.8 2.9 fusion.115
  327.2 20.3 %all_to_all.41 = f32[1,240,512]{1,0,2:T(1,128)S(1)} all-to-all(f32[1,240,512]{1,0,2:T(1,128)S(1)} %copy.233), channel_id=1, replica_groups=mesh['seq'=32,'chan'=8] {'seq'}, dimensions={2} | all-to-all | bytes 983040 | tf_op jit(solution)/shard_map/all_to_all | solution.py:85
  354.0 54.0 %all_to_all.42 = f32[2,1,2,240,512]{3,2,1,0,4:T(2,128)S(1)} all-to-all(f32[2,1,2,240,512]{3,2,1,0,4:T(2,128)S(1)} %copy.238), channel_id=1, replica_groups=mesh['seq'=32,'chan'=8] {'seq'}, dimensions={4} | all-to-all | bytes 3932160 | tf_op jit(solution)/shard_map/all_to_all | solution.py:89
  413.8 1.9 subtract_bitcast_fusion.2
  419.2 1.9 fusion.63
  425.1 4.4 multiply_add_fusion.1
  429.4 2.0 fusion.36
  431.5 2.3 fusion.37
  433.7 2.1 fusion.40
  435.9 2.7 fusion.2
  438.6 3.3 fusion.12
  441.9 3.3 fusion.14
  445.2 3.9 subtract_bitcast_fusion
  449.1 3.4 add_bitcast_fusion
  455.8 5.4 copy.273
  461.2 5.0 all-to-all-start.6
  466.3 2.0 fusion.118
  468.4 108.0 %all-to-all-done.6 = f32[2,2,2,240,512]{3,2,1,0,4:T(2,128)} async-done(((f32[2,2,2,240,512]{3,2,1,0,4:T(2,128)}), f32[2,2,2,240,512]{3,2,1,0,4:T(2,128)}, u32[]{:S(2)}, u32[]{:S(2)}) %all-to-all-start.6) | async-done | bytes 3932192 | tf_op jit(solution)/shard_map/all_to_all | solution.py:89
  576.4 3.7 fusion.729
  580.9 2.7 fusion.56
  583.6 2.7 fusion.73
  586.9 1.8 copy.279
  588.7 5.6 all-to-all-start.7
  594.3 163.5 %all-reduce.2.cloned.1.call-done = f32[240,1920]{0,1:T(8,128)} async-done(((f32[240,1920]{0,1:T(8,128)}), f32[240,1920]{0,1:T(8,128)}) %all-reduce.2.cloned.1.call-update) | async-done | bytes 1843216 | tf_op jit(solution)/shard_map/psum | solution.py:186
  (110 shorter events, 57.0 us)
Async XLA Ops:
  7.2 316.7 %copy-start = (bf16[240,1920]{1,0:T(8,128)(2,1)S(1)}, bf16[240,1920]{1,0:T(8,128)(2,1)}, u32[]{:S(2)}) copy-start(bf16[240,1920]{1,0:T(8,128)(2,1)} %param.12) | copy-start | bytes 2764804
  10.9 36.7 %all-to-all-start = ((f32[2,240,512]{1,0,2:T(2,128)}), f32[2,240,512]{1,0,2:T(2,128)S(1)}, u32[]{:S(2)}, u32[]{:S(2)}) async-start(f32[2,240,512]{1,0,2:T(2,128)} %copy.196), calls=%async_computation | async-start | bytes 2097152 | tf_op jit(solution)/shard_map/all_to_all | solution.py:85
  61.9 100.3 %all-to-all-start.1 = ((f32[2,2,2,240,512]{3,2,1,0,4:T(2,128)}), f32[2,2,2,240,512]{3,2,1,0,4:T(2,128)}, u32[]{:S(2)}, u32[]{:S(2)}) async-start(f32[2,2,2,240,512]{3,2,1,0,4:T(2,128)} %copy.202), calls=%async_computation.1 | async-start | bytes 8388608 | tf_op jit(solution)/shard_map/all_to_all | solution.py:89
  217.5 80.8 %all-to-all-start.2 = ((f32[2,1,2,240,512]{3,2,1,0,4:T(2,128)}), f32[2,1,2,240,512]{3,2,1,0,4:T(2,128)S(1)}, u32[]{:S(2)}, u32[]{:S(2)}) async-start(f32[2,1,2,240,512]{3,2,1,0,4:T(2,128)} %copy.225), calls=%async_computation.2 | async-start | bytes 4194304 | tf_op jit(solution)/shard_map/all_to_all | solution.py:89
  221.5 102.3 %all-gather.2.cloned.1.call-start = ((), (), s32[]{:S(2)}) async-start(), calls=%async_computation.8 | async-start | bytes 2211840 | tf_op jit(solution)/shard_map/all_gather | solution.py:177
  302.2 21.6 %copy-start.7 = (bf16[240,512]{1,0:T(8,128)(2,1)S(1)}, bf16[240,512]{1,0:T(8,128)(2,1)}, u32[]{:S(2)}) copy-start(bf16[240,512]{1,0:T(8,128)(2,1)} %param.7) | copy-start | bytes 737284
  422.9 1.3 copy-start.3
  422.9 1.5 copy-start.4
  422.9 1.8 copy-start.5
  422.9 2.1 copy-start.6
  461.2 5.1 copy-start.2
  461.2 5.1 copy-start.8
  461.2 115.1 %all-to-all-start.6 = ((f32[2,2,2,240,512]{3,2,1,0,4:T(2,128)}), f32[2,2,2,240,512]{3,2,1,0,4:T(2,128)}, u32[]{:S(2)}, u32[]{:S(2)}) async-start(f32[2,2,2,240,512]{3,2,1,0,4:T(2,128)} %copy.273), calls=%async_computation.6 | async-start | bytes 8388608 | tf_op jit(solution)/shard_map/all_to_all | solution.py:89
  466.2 291.6 %all-reduce.2.cloned.1.call-start = ((), (), s32[]{:S(2)}) async-start(), calls=%async_computation.9 | async-start | bytes 3932160 | tf_op jit(solution)/shard_map/psum | solution.py:186
  588.7 170.6 %all-to-all-start.7 = ((f32[2,240,512]{1,0,2:T(2,128)}), f32[2,240,512]{1,0,2:T(2,128)S(1)}, u32[]{:S(2)}, u32[]{:S(2)}) async-start(f32[2,240,512]{1,0,2:T(2,128)} %copy.279), calls=%async_computation.7 | async-start | bytes 2097152 | tf_op jit(solution)/shard_map/all_to_all | solution.py:85
  759.3 2.5 copy-start.9
  759.3 2.5 copy-start.10
  760.1 2.5 copy-start.1
Sparse Core Ops, SparseCore 0:
  225.0 73.2 all-gather.1
  469.7 288.0 all-reduce.1
where the time goes:
time: 780 us; the launch traced here: 770 us
  waiting for transfers between devices  470 us (60%)
  matrix products  100 us (13%)
  blocking collectives  94.7 us (12%)
  local copies, waits for them, and re-layouts  47.2 us (6%)
  starting transfers between devices  28.3 us (4%)
  between operations  15.1 us (2%)
  other arithmetic  14 us (2%)
    all_to_all x3, waiting for transfers between devices, exchange_frequencies(): lax.all_to_all(spectral_rows, 'seq', split_axis=4, concat_axis=4, tiled=T...  279 us
    psum x1, waiting for transfers between devices, per_device(): summed = lax.psum(partial_value, 'seq')  163 us
    all_to_all x1, blocking collectives, exchange_frequencies(): lax.all_to_all(spectral_rows, 'seq', split_axis=4, concat_axis=4, tiled=T...  54 us
    all_to_all x2, blocking collectives, exchange_tokens(): lax.all_to_all(token_rows, 'seq', split_axis=2, concat_axis=2, tiled=True)  40.7 us
    all_to_all x2, waiting for transfers between devices, exchange_tokens(): lax.all_to_all(token_rows, 'seq', split_axis=2, concat_axis=2, tiled=True)  27.1 us
    dot_general x8, matrix products, apply_table(): jnp.einsum(form, sine_part, signal_pair[0], precision=precise)  20.4 us
    dot_general x8, matrix products, apply_table(): jnp.einsum(form, cosine, signal_pair[0], precision=precise)  20 us
    dot_general x8, matrix products, apply_table(): jnp.einsum(form, sine_part, signal_pair[1], precision=precise)  19.4 us
  transfers between devices with their start and end apart: 7, of which 5 were waited for; matrix products, arithmetic and copies ran while one was open for 3% of the time, Pallas kernels for 0%

commit v1 on v0

v1 whole, which is shorter than its diff:
```python
import functools
import math

import jax
import jax.numpy as jnp
import numpy as np
from jax import lax
from jax.experimental import pallas as pl
from jax.experimental.pallas import tpu as pltpu
from jax.sharding import PartitionSpec as P

F32 = jnp.float32
BF16 = jnp.bfloat16
SIDE = 128
LENGTH = SIDE * SIDE
OWNED = 8


def halves(table):
    high = np.asarray(table, np.float32).astype(jnp.bfloat16)
    low = (np.asarray(table, np.float64) - high.astype(np.float64)).astype(np.float32).astype(jnp.bfloat16)
    return high, low


def make_tables():
    n = np.arange(SIDE, dtype=np.float64)
    outer = 2.0 * np.pi * np.outer(n + 0.25, n) / SIDE
    first = np.concatenate([np.cos(outer), -np.sin(outer)], 0)
    first_high, first_low = halves(first)
    first_both = np.concatenate([first_high, first_low], 1)
    turn = 2.0 * np.pi * np.outer(n + 0.25, n) / LENGTH
    twist = np.stack([np.cos(turn), np.sin(turn)]).astype(np.float32)
    inner = 2.0 * np.pi * np.outer(n, n) / SIDE
    cosine, sine = np.cos(inner), np.sin(inner)
    forward = np.concatenate([np.concatenate([cosine, -sine], 1), np.concatenate([sine, cosine], 1)], 0)
    backward = np.concatenate([np.concatenate([cosine, sine], 1), np.concatenate([-sine, cosine], 1)], 0)
    last = np.concatenate([np.cos(outer.T), -np.sin(outer.T)], 1) / LENGTH
    return (
        first_both,
        twist,
        np.stack(halves(forward)),
        np.stack(halves(backward)),
        np.stack(halves(last)),
    )


def dot(a, b):
    return jnp.dot(a, b, preferred_element_type=F32)


def split(x):
    high = x.astype(BF16)
    return high, (x - high.astype(F32)).astype(BF16)


def forward_pair(x, first, twist, forward, count):
    a = dot(first[...], jnp.concatenate([x, x], 0))
    cosine, sine = twist[0], twist[1]
    rows = []
    for i in range(count):
        real = a[:SIDE, i * SIDE : (i + 1) * SIDE]
        imag = a[SIDE:, i * SIDE : (i + 1) * SIDE]
        rows.append(jnp.concatenate([real * cosine + imag * sine, imag * cosine - real * sine], 1))
    high, low = split(jnp.concatenate(rows, 0))
    return dot(high, forward[0]) + dot(high, forward[1]) + dot(low, forward[0])


def backward_pair(spec, twist, backward, last, count):
    high, low = split(spec)
    d = dot(high, backward[0]) + dot(high, backward[1]) + dot(low, backward[0])
    cosine, sine = twist[0], twist[1]
    columns = []
    for i in range(count):
        real = d[i * SIDE : (i + 1) * SIDE, :SIDE]
        imag = d[i * SIDE : (i + 1) * SIDE, SIDE:]
        columns.append(jnp.concatenate([real * cosine - imag * sine, imag * cosine + real * sine], 0))
    high, low = split(jnp.concatenate(columns, 1))
    return dot(last[0], high) + dot(last[1], high) + dot(last[0], low)


def product(a, b):
    ar, ai, br, bi = a[:, :SIDE], a[:, SIDE:], b[:, :SIDE], b[:, SIDE:]
    return jnp.concatenate([ar * br - ai * bi, ar * bi + ai * br], 1)


def product_conj(a, b):
    ar, ai, br, bi = a[:, :SIDE], a[:, SIDE:], b[:, :SIDE], b[:, SIDE:]
    return jnp.concatenate([ar * br + ai * bi, ar * bi - ai * br], 1)


def transform_kernel(sig, ker, gr, first, twist, forward, backward, last, conv, sgrad, kgrad):
    for c in range(OWNED):
        x = jnp.concatenate([sig[c], ker[c]], 1)
        spec = forward_pair(x, first, twist, forward, 2)
        sspec, kspec = spec[:SIDE], spec[SIDE:]
        conv[c] = backward_pair(product(sspec, kspec), twist, backward, last, 1).astype(BF16)
        gspec = forward_pair(gr[c], first, twist, forward, 1)
        both = jnp.concatenate([product_conj(kspec, gspec), product_conj(sspec, gspec)], 0)
        y = backward_pair(both, twist, backward, last, 2)
        sgrad[c] = y[:, :SIDE].astype(BF16)
        kgrad[c] = y[:, SIDE:].astype(BF16)


def convolve(sig, ker, gr):
    tables = [jnp.asarray(t) for t in make_tables()]
    shape = jax.ShapeDtypeStruct((OWNED, SIDE, SIDE), BF16)
    return pl.pallas_call(
        transform_kernel,
        out_shape=(shape,) * 3,
        compiler_params=pltpu.CompilerParams(vmem_limit_bytes=32 * 2**20),
    )(sig, ker, gr, *tables)


def gather_rows(x):
    pieces = lax.axis_size("seq")
    channels, length = x.shape
    x = jnp.pad(x, ((0, OWNED * pieces - channels), (0, 0)))
    y = lax.all_to_all(x.reshape(pieces, OWNED, length), "seq", split_axis=0, concat_axis=0, tiled=True)
    return y.reshape(pieces, OWNED, length // SIDE, SIDE).transpose(1, 0, 2, 3).reshape(OWNED, SIDE, SIDE)


def scatter_rows(y, channels, length):
    pieces = lax.axis_size("seq")
    x = y.reshape(OWNED, pieces, length // SIDE, SIDE).transpose(1, 0, 2, 3).reshape(pieces, OWNED, length)
    x = lax.all_to_all(x, "seq", split_axis=0, concat_axis=0, tiled=True)
    return x.reshape(pieces * OWNED, length)[:channels].astype(F32)


def per_device(gate_act, key_act, value_act, filter_raw, decay_rate, out_weight, out_grad):
    channels, length = gate_act.shape
    device_index = lax.axis_index("seq")
    position = (device_index * length + lax.iota(jnp.int32, length)).astype(F32)
    envelope = jnp.sqrt(1.0 - jnp.exp(-2.0 * decay_rate))[:, None] * jnp.exp(
        -decay_rate[:, None] * position[None, :]
    )
    kernel = (filter_raw * envelope).astype(BF16)
    gate_full = gate_act.astype(F32)
    key_full = key_act.astype(F32)
    value_full = value_act.astype(F32)
    signal = (key_full * value_full).astype(BF16)
    everything = lax.all_gather(out_grad, "chan", axis=0, tiled=True)
    sig = gather_rows(signal)
    ker = gather_rows(kernel)
    upstream = jnp.dot(out_weight, everything, preferred_element_type=F32)
    gr = gather_rows((upstream * gate_full).astype(BF16))
    conv, sgrad, kgrad = convolve(sig, ker, gr)
    conv = scatter_rows(conv, channels, length)
    sgrad = scatter_rows(sgrad, channels, length)
    kgrad = scatter_rows(kgrad, channels, length)
    gated = (gate_full * conv).astype(BF16)
    partial = lax.dot_general(gated, everything, (((1,), (1,)), ((), ())), preferred_element_type=F32)
    pieces = lax.axis_size("seq")
    partial = partial.reshape(channels, pieces, -1).transpose(1, 0, 2)
    weight_grad = lax.psum_scatter(partial, "seq", scatter_dimension=0, tiled=False)
    return (
        (upstream * conv).astype(BF16),
        (sgrad * value_full).astype(BF16),
        (sgrad * key_full).astype(BF16),
        kgrad * envelope,
        weight_grad,
    )


def solution(mesh):
    rows = P("chan", "seq")
    return jax.shard_map(
        per_device,
        mesh=mesh,
        in_specs=(rows, rows, rows, rows, P("chan"), P("chan", None), rows),
        out_specs=(rows,) * 5,
        check_vma=False,
    )
```

time: 780 us -> 290 us (0.37); the launches traced: 770 us -> 290 us
  waiting for transfers between devices: 470 us -> 207 us
  matrix products: 100 us -> 5.42 us
  blocking collectives: 94.7 us -> 14.7 us
  local copies, waits for them, and re-layouts: 47.2 us -> 7.15 us
  Pallas kernels: 0 us -> 11.6 us
  other arithmetic: 14 us -> 4.55 us
    all_to_all x5, waiting for transfers between devices: 306 us -> 41.8 us  [the longest x3 21 us: gather_rows(): lax.all_to_all(x.reshape(pieces, OWNED, length), 'seq', split_axis=0, con...]
    psum x1 -> x0, waiting for transfers between devices: 163 us -> none  [per_device(): summed = lax.psum(partial_value, 'seq')]
    reduce_scatter x0 -> x1, waiting for transfers between devices: none -> 112 us  [per_device(): lax.psum_scatter(partial, 'seq', scatter_dimension=0, tiled=False)]
    dot_general x42 -> x2, matrix products: 100 us -> 5.42 us  [the longest x1 3.01 us: per_device(): upstream = jnp.dot(out_weight, everything, preferred_element_type=F32)]
    all_to_all x3 -> x1, blocking collectives: 94.7 us -> 14.7 us  [scatter_rows(): x = lax.all_to_all(x, 'seq', split_axis=0, concat_axis=0, tiled=True)]
    all_gather x1, waiting for transfers between devices: 0.02 us -> 52 us  [per_device(): everything = lax.all_gather(out_grad, 'chan', axis=0, tiled=True)]
    another operation x5 -> x0, local copies, waits for them, and re-layouts: 17 us -> none  [the longest x4 15.6 us: rotate(): jnp.stack([signal_pair[0] * cosine - signal_pair[1] * sine_part, signal_p...]
    pallas_call x0 -> x1, Pallas kernels: none -> 11.6 us  [convolve(): pl.pallas_call(transform_kernel, out_shape=(shape,) * 3, compiler_params=...]
  transfers between devices with their start and end apart: 7 -> 7, of which waited for: 5 -> 6; matrix products, arithmetic and copies ran while one was open for 3% -> 4% of each run, Pallas kernels for 0% -> 0%
where the time goes in v1:
time: 290 us
  waiting for transfers between devices  207 us (71%)
  starting transfers between devices  25.3 us (9%)
  blocking collectives  14.7 us (5%)
  between operations  14.3 us (5%)
  Pallas kernels  11.6 us (4%)
  local copies, waits for them, and re-layouts  7.15 us (2%)
  matrix products  5.42 us (2%)
  other arithmetic  4.55 us (2%)
    reduce_scatter x1, waiting for transfers between devices, per_device(): lax.psum_scatter(partial, 'seq', scatter_dimension=0, tiled=False)  112 us
    all_gather x1, waiting for transfers between devices, per_device(): everything = lax.all_gather(out_grad, 'chan', axis=0, tiled=True)  52 us
    all_to_all x3, waiting for transfers between devices, gather_rows(): lax.all_to_all(x.reshape(pieces, OWNED, length), 'seq', split_axis=0, con...  21 us
    all_to_all x2, waiting for transfers between devices, scatter_rows(): x = lax.all_to_all(x, 'seq', split_axis=0, concat_axis=0, tiled=True)  20.8 us
    all_to_all x3, starting transfers between devices, gather_rows(): lax.all_to_all(x.reshape(pieces, OWNED, length), 'seq', split_axis=0, con...  17.3 us
    all_to_all x1, blocking collectives, scatter_rows(): x = lax.all_to_all(x, 'seq', split_axis=0, concat_axis=0, tiled=True)  14.7 us
    pallas_call x1, Pallas kernels, convolve(): pl.pallas_call(transform_kernel, out_shape=(shape,) * 3, compiler_params=...  11.6 us
    all_to_all x2, starting transfers between devices, scatter_rows(): x = lax.all_to_all(x, 'seq', split_axis=0, concat_axis=0, tiled=True)  7.96 us
  transfers between devices with their start and end apart: 7, of which 6 were waited for; matrix products, arithmetic and copies ran while one was open for 4% of the time, Pallas kernels for 0%

profile of v1, /device:TPU:16, one launch (start us, length us, event | category | flops | bytes accessed | tf_op | source)
XLA Modules:
  0.0 289.8 jit_solution(1474550117110685636)
XLA Ops:
  7.2 0.0 copy-start
  7.2 0.0 copy-start.10
  7.2 0.0 copy-start.12
  7.2 0.0 copy-start.9
  7.2 0.0 all-gather.2.cloned.1.call-start
  7.3 0.7 all-gather.2.cloned.1.call-update
  8.0 0.7 subtract_sqrt_fusion
  8.7 1.2 multiply_convert_fusion
  9.9 0.7 pad_bitcast_fusion.1
  10.6 8.8 %all-to-all-start.1 = ((bf16[32,8,512]{2,1,0:T(8,128)(2,1)}), bf16[32,8,512]{2,1,0:T(8,128)(2,1)S(1)}, u32[]{:S(2)}, u32[]{:S(2)}) async-start(bf16[32,8,512]{2,1,0:T(8,128)(2,1)} %pad_bitcast_fusion.1), calls=%async_computation.1 | async-start | bytes 524288 | tf_op jit(solution)/shard_map/all_to_all | solution.py:118
  19.4 0.1 fusion
  19.4 0.7 pad_bitcast_fusion.2
  20.2 10.3 %all-to-all-done.1 = bf16[32,8,512]{2,1,0:T(8,128)(2,1)S(1)} async-done(((bf16[32,8,512]{2,1,0:T(8,128)(2,1)}), bf16[32,8,512]{2,1,0:T(8,128)(2,1)S(1)}, u32[]{:S(2)}, u32[]{:S(2)}) %all-to-all-start.1) | async-done | bytes 262176 | tf_op jit(solution)/shard_map/all_to_all | solution.py:118
  30.4 3.9 %all-to-all-start = ((bf16[32,8,512]{2,1,0:T(8,128)(2,1)}), bf16[32,8,512]{2,1,0:T(8,128)(2,1)S(1)}, u32[]{:S(2)}, u32[]{:S(2)}) async-start(bf16[32,8,512]{2,1,0:T(8,128)(2,1)} %pad_bitcast_fusion.2), calls=%async_computation | async-start | bytes 524288 | tf_op jit(solution)/shard_map/all_to_all | solution.py:118
  34.3 52.0 %all-gather.2.cloned.1.call-done = bf16[1920,512]{1,0:T(8,128)(2,1)} async-done(((bf16[240,512]{1,0:T(8,128)(2,1)}), bf16[1920,512]{1,0:T(8,128)(2,1)}) %all-gather.2.cloned.1.call-update) | async-done | bytes 1966096 | tf_op jit(solution)/shard_map/all_gather | solution.py:141
  86.4 3.0 %fusion.1 = (bf16[240,512]{1,0:T(8,128)(2,1)S(1)}, f32[240,512]{1,0:T(8,128)}) fusion(bf16[240,512]{1,0:T(8,128)(2,1)S(1)} %copy-done.9, bf16[240,1920]{1,0:T(8,128)(2,1)S(1)} %copy-done, bf16[1920,512]{1,0:T(8,128)(2,1)} %all-gather.2.cloned.1.call-done), kind=kOutput, calls=%fused_computation.7 | convolution fusion | flops 472227840 | bytes 3870720 | tf_op jit(solution)/shard_map/dot_general | solution.py:144
  89.4 0.0 copy-start.5
  89.4 0.7 pad_bitcast_fusion
  90.2 0.0 all-to-all-done
  90.2 4.6 %all-to-all-start.2 = ((bf16[32,8,512]{2,1,0:T(8,128)(2,1)}), bf16[32,8,512]{2,1,0:T(8,128)(2,1)S(1)}, u32[]{:S(2)}, u32[]{:S(2)}) async-start(bf16[32,8,512]{2,1,0:T(8,128)(2,1)} %pad_bitcast_fusion), calls=%async_computation.2 | async-start | bytes 524288 | tf_op jit(solution)/shard_map/all_to_all | solution.py:118
  94.8 0.0 reduce-scatter.2.cloned.1.call-start
  94.9 0.1 reshape.98
  94.9 0.1 copy.33
  95.0 0.1 reshape.97
  95.1 0.1 copy.32
  95.2 10.7 %all-to-all-done.2 = bf16[32,8,512]{2,1,0:T(8,128)(2,1)S(1)} async-done(((bf16[32,8,512]{2,1,0:T(8,128)(2,1)}), bf16[32,8,512]{2,1,0:T(8,128)(2,1)S(1)}, u32[]{:S(2)}, u32[]{:S(2)}) %all-to-all-start.2) | async-done | bytes 262176 | tf_op jit(solution)/shard_map/all_to_all | solution.py:118
  105.9 0.1 reshape.99
  106.0 0.1 copy.34
  106.1 11.6 %shard_map.155 = (bf16[8,128,128]{2,1,0:T(8,128)(2,1)S(1)}, bf16[8,128,128]{2,1,0:T(8,128)(2,1)S(1)}, bf16[8,128,128]{2,1,0:T(8,128)(2,1)S(1)}) custom-call(bf16[8,128,128]{2,1,0:T(8,128)(2,1)S(1)} %bitcast.58, bf16[8,128,128]{2,1,0:T(8,128)(2,1)S(1)} %bitcast.57, bf16[8,128,128]{2,1,0:T(8,128)(2,1)S(1)} %bitcast.59, bf16[256,256]{1,0:T(8,128)(2,1)S(1)} %copy-done.5, ...), custom_call_target="tpu_custom_call" | custom-call | tf_op jit(solution)/shard_map/pallas_call | solution.py:107
  117.7 0.1 reshape.88
  117.8 0.2 copy.27
  118.0 14.7 %all_to_all.30 = bf16[32,8,512]{2,1,0:T(8,128)(2,1)S(1)} all-to-all(bf16[32,8,512]{2,1,0:T(8,128)(2,1)S(1)} %copy.27), channel_id=1, replica_groups=mesh['seq'=32,'chan'=8] {'seq'}, dimensions={0} | all-to-all | bytes 524288 | tf_op jit(solution)/shard_map/all_to_all | solution.py:125
  132.7 0.7 copy-done.6
  133.4 2.4 fusion.6
  135.8 1.5 reshape.93
  137.4 0.0 reduce-scatter.2.cloned.1.call-update
  137.4 0.1 reshape.92
  137.5 0.9 copy.29
  138.4 4.0 %all-to-all-start.5 = ((bf16[32,8,512]{2,1,0:T(8,128)(2,1)}), bf16[32,8,512]{2,1,0:T(8,128)(2,1)S(1)}, u32[]{:S(2)}, u32[]{:S(2)}) async-start(bf16[32,8,512]{2,1,0:T(8,128)(2,1)} %copy.29), calls=%async_computation.5 | async-start | bytes 524288 | tf_op jit(solution)/shard_map/all_to_all | solution.py:125
  142.4 0.1 reshape.90
  142.5 0.9 copy.28
  143.3 10.6 %all-to-all-done.5 = bf16[32,8,512]{2,1,0:T(8,128)(2,1)S(1)} async-done(((bf16[32,8,512]{2,1,0:T(8,128)(2,1)}), bf16[32,8,512]{2,1,0:T(8,128)(2,1)S(1)}, u32[]{:S(2)}, u32[]{:S(2)}) %all-to-all-start.5) | async-done | bytes 262176 | tf_op jit(solution)/shard_map/all_to_all | solution.py:125
  153.9 4.0 %all-to-all-start.4 = ((bf16[32,8,512]{2,1,0:T(8,128)(2,1)}), bf16[32,8,512]{2,1,0:T(8,128)(2,1)S(1)}, u32[]{:S(2)}, u32[]{:S(2)}) async-start(bf16[32,8,512]{2,1,0:T(8,128)(2,1)} %copy.28), calls=%async_computation.4 | async-start | bytes 524288 | tf_op jit(solution)/shard_map/all_to_all | solution.py:125
  157.9 0.9 convert_multiply_fusion.6
  158.9 0.8 fusion.4
  159.6 10.2 %all-to-all-done.4 = bf16[32,8,512]{2,1,0:T(8,128)(2,1)S(1)} async-done(((bf16[32,8,512]{2,1,0:T(8,128)(2,1)}), bf16[32,8,512]{2,1,0:T(8,128)(2,1)S(1)}, u32[]{:S(2)}, u32[]{:S(2)}) %all-to-all-start.4) | async-done | bytes 262176 | tf_op jit(solution)/shard_map/all_to_all | solution.py:125
  169.8 0.9 fusion.3
  170.7 112.3 %reduce-scatter.2.cloned.1.call-done = f32[1,240,60]{1,2,0:T(8,128)} async-done(((f32[32,240,60]{1,2,0:T(8,128)}), f32[1,240,60]{1,2,0:T(8,128)}) %reduce-scatter.2.cloned.1.call-update) | async-done | bytes 57616 | tf_op jit(solution)/shard_map/reduce_scatter | solution.py:154
  (23 shorter events, 0.0 us)
Async XLA Ops:
  7.2 79.2 %copy-start = (bf16[240,1920]{1,0:T(8,128)(2,1)S(1)}, bf16[240,1920]{1,0:T(8,128)(2,1)}, u32[]{:S(2)}) copy-start(bf16[240,1920]{1,0:T(8,128)(2,1)} %param.17) | copy-start | bytes 2764804
  7.2 12.2 %copy-start.10 = (bf16[240,512]{1,0:T(8,128)(2,1)S(1)}, bf16[240,512]{1,0:T(8,128)(2,1)}, u32[]{:S(2)}) copy-start(bf16[240,512]{1,0:T(8,128)(2,1)} %param.14) | copy-start | bytes 737284
  7.2 12.2 %copy-start.12 = (bf16[240,512]{1,0:T(8,128)(2,1)S(1)}, bf16[240,512]{1,0:T(8,128)(2,1)}, u32[]{:S(2)}) copy-start(bf16[240,512]{1,0:T(8,128)(2,1)} %param.13) | copy-start | bytes 737284
  7.2 79.2 %copy-start.9 = (bf16[240,512]{1,0:T(8,128)(2,1)S(1)}, bf16[240,512]{1,0:T(8,128)(2,1)}, u32[]{:S(2)}) copy-start(bf16[240,512]{1,0:T(8,128)(2,1)} %param.12) | copy-start | bytes 737284
  7.2 79.2 %all-gather.2.cloned.1.call-start = ((), (), s32[]{:S(2)}) async-start(), calls=%async_computation.7 | async-start | bytes 2211840 | tf_op jit(solution)/shard_map/all_gather | solution.py:141
  10.6 19.9 %all-to-all-start.1 = ((bf16[32,8,512]{2,1,0:T(8,128)(2,1)}), bf16[32,8,512]{2,1,0:T(8,128)(2,1)S(1)}, u32[]{:S(2)}, u32[]{:S(2)}) async-start(bf16[32,8,512]{2,1,0:T(8,128)(2,1)} %pad_bitcast_fusion.1), calls=%async_computation.1 | async-start | bytes 524288 | tf_op jit(solution)/shard_map/all_to_all | solution.py:118
  30.4 59.7 %all-to-all-start = ((bf16[32,8,512]{2,1,0:T(8,128)(2,1)}), bf16[32,8,512]{2,1,0:T(8,128)(2,1)S(1)}, u32[]{:S(2)}, u32[]{:S(2)}) async-start(bf16[32,8,512]{2,1,0:T(8,128)(2,1)} %pad_bitcast_fusion.2), calls=%async_computation | async-start | bytes 524288 | tf_op jit(solution)/shard_map/all_to_all | solution.py:118
  89.4 16.7 %copy-start.1 = (bf16[2,256,256]{2,1,0:T(8,128)(2,1)S(1)}, bf16[2,256,256]{2,1,0:T(8,128)(2,1)}, u32[]{:S(2)}) copy-start(bf16[2,256,256]{2,1,0:T(8,128)(2,1)} %constant.28.clone.backward) | copy-start | bytes 786436
  89.4 16.7 %copy-start.2 = (bf16[2,256,256]{2,1,0:T(8,128)(2,1)S(1)}, bf16[2,256,256]{2,1,0:T(8,128)(2,1)}, u32[]{:S(2)}) copy-start(bf16[2,256,256]{2,1,0:T(8,128)(2,1)} %constant.27.clone.forward) | copy-start | bytes 786436
  89.4 16.7 %copy-start.3 = (bf16[2,128,256]{2,1,0:T(8,128)(2,1)S(1)}, bf16[2,128,256]{2,1,0:T(8,128)(2,1)}, u32[]{:S(2)}) copy-start(bf16[2,128,256]{2,1,0:T(8,128)(2,1)} %constant.29.clone.last) | copy-start | bytes 393220
  89.4 16.7 %copy-start.4 = (f32[2,128,128]{2,1,0:T(8,128)S(1)}, f32[2,128,128]{2,1,0:T(8,128)}, u32[]{:S(2)}) copy-start(f32[2,128,128]{2,1,0:T(8,128)} %constant.26.clone.twist) | copy-start | bytes 393220
  89.4 16.7 %copy-start.5 = (bf16[256,256]{1,0:T(8,128)(2,1)S(1)}, bf16[256,256]{1,0:T(8,128)(2,1)}, u32[]{:S(2)}) copy-start(bf16[256,256]{1,0:T(8,128)(2,1)} %constant.25.clone.first) | copy-start | bytes 393220
  90.2 15.8 %all-to-all-start.2 = ((bf16[32,8,512]{2,1,0:T(8,128)(2,1)}), bf16[32,8,512]{2,1,0:T(8,128)(2,1)S(1)}, u32[]{:S(2)}, u32[]{:S(2)}) async-start(bf16[32,8,512]{2,1,0:T(8,128)(2,1)} %pad_bitcast_fusion), calls=%async_computation.2 | async-start | bytes 524288 | tf_op jit(solution)/shard_map/all_to_all | solution.py:118
  94.8 188.2 %reduce-scatter.2.cloned.1.call-start = ((), (), s32[]{:S(2)}) async-start(), calls=%async_computation.8 | async-start | bytes 2162688 | tf_op jit(solution)/shard_map/reduce_scatter | solution.py:154
  132.7 0.7 copy-start.6
  137.4 21.5 %copy-start.7 = (bf16[32,8,512]{2,1,0:T(8,128)(2,1)S(1)}, bf16[32,8,512]{2,1,0:T(8,128)(2,1)}, u32[]{:S(2)}) copy-start(bf16[32,8,512]{2,1,0:T(8,128)(2,1)} %copy-done.6) | copy-start | bytes 786436
  137.4 21.5 %copy-start.8 = (f32[240,512]{1,0:T(8,128)S(1)}, f32[240,512]{1,0:T(8,128)}, u32[]{:S(2)}) copy-start(f32[240,512]{1,0:T(8,128)} %get-tuple-element.16) | copy-start | bytes 1474564
  138.4 31.4 %copy-start.11 = (bf16[240,512]{1,0:T(8,128)(2,1)S(1)}, bf16[240,512]{1,0:T(8,128)(2,1)}, u32[]{:S(2)}) copy-start(bf16[240,512]{1,0:T(8,128)(2,1)} %param.14) | copy-start | bytes 737284
  138.4 31.4 %copy-start.13 = (bf16[240,512]{1,0:T(8,128)(2,1)S(1)}, bf16[240,512]{1,0:T(8,128)(2,1)}, u32[]{:S(2)}) copy-start(bf16[240,512]{1,0:T(8,128)(2,1)} %param.13) | copy-start | bytes 737284
  138.4 15.6 %all-to-all-start.5 = ((bf16[32,8,512]{2,1,0:T(8,128)(2,1)}), bf16[32,8,512]{2,1,0:T(8,128)(2,1)S(1)}, u32[]{:S(2)}, u32[]{:S(2)}) async-start(bf16[32,8,512]{2,1,0:T(8,128)(2,1)} %copy.29), calls=%async_computation.5 | async-start | bytes 524288 | tf_op jit(solution)/shard_map/all_to_all | solution.py:125
  153.9 15.9 %all-to-all-start.4 = ((bf16[32,8,512]{2,1,0:T(8,128)(2,1)}), bf16[32,8,512]{2,1,0:T(8,128)(2,1)S(1)}, u32[]{:S(2)}, u32[]{:S(2)}) async-start(bf16[32,8,512]{2,1,0:T(8,128)(2,1)} %copy.28), calls=%async_computation.4 | async-start | bytes 524288 | tf_op jit(solution)/shard_map/all_to_all | solution.py:125
Sparse Core Ops, SparseCore 0:
  10.7 75.6 all-gather.1
  137.5 145.4 reduce-scatter.1

commit v2 on v1

v2 whole, which is shorter than its diff:
```python
import functools
import math

import jax
import jax.numpy as jnp
import numpy as np
from jax import lax
from jax.experimental import pallas as pl
from jax.experimental.pallas import tpu as pltpu
from jax.sharding import PartitionSpec as P

F32 = jnp.float32
BF16 = jnp.bfloat16
SIDE = 128
LENGTH = SIDE * SIDE
OWNED = 8
PIECES = 32
GROUPS = 8
HALF = 256


def halves(table):
    high = np.asarray(table, np.float32).astype(jnp.bfloat16)
    low = (np.asarray(table, np.float64) - high.astype(np.float64)).astype(np.float32).astype(jnp.bfloat16)
    return high, low


def make_tables():
    n = np.arange(SIDE, dtype=np.float64)
    outer = 2.0 * np.pi * np.outer(n + 0.25, n) / SIDE
    first = np.concatenate([np.cos(outer), -np.sin(outer)], 0)
    first_high, first_low = halves(first)
    first_both = np.concatenate([first_high, first_low], 1)
    turn = 2.0 * np.pi * np.outer(n + 0.25, n) / LENGTH
    twist = np.stack([np.cos(turn), np.sin(turn)]).astype(np.float32)
    inner = 2.0 * np.pi * np.outer(n, n) / SIDE
    cosine, sine = np.cos(inner), np.sin(inner)
    forward = np.concatenate([np.concatenate([cosine, -sine], 1), np.concatenate([sine, cosine], 1)], 0)
    backward = np.concatenate([np.concatenate([cosine, sine], 1), np.concatenate([-sine, cosine], 1)], 0)
    last = np.concatenate([np.cos(outer.T), -np.sin(outer.T)], 1) / LENGTH
    return (
        first_both,
        twist,
        np.stack(halves(forward)),
        np.stack(halves(backward)),
        np.stack(halves(last)),
    )


def dot(a, b):
    return jnp.dot(a, b, preferred_element_type=F32)


def split(x):
    high = x.astype(BF16)
    return high, (x - high.astype(F32)).astype(BF16)


def forward_pair(x, first, twist, forward, count):
    a = dot(first[...], jnp.concatenate([x, x], 0))
    cosine, sine = twist[0], twist[1]
    rows = []
    for i in range(count):
        real = a[:SIDE, i * SIDE : (i + 1) * SIDE]
        imag = a[SIDE:, i * SIDE : (i + 1) * SIDE]
        rows.append(jnp.concatenate([real * cosine + imag * sine, imag * cosine - real * sine], 1))
    high, low = split(jnp.concatenate(rows, 0))
    return dot(high, forward[0]) + dot(high, forward[1]) + dot(low, forward[0])


def backward_pair(spec, twist, backward, last, count):
    high, low = split(spec)
    d = dot(high, backward[0]) + dot(high, backward[1]) + dot(low, backward[0])
    cosine, sine = twist[0], twist[1]
    columns = []
    for i in range(count):
        real = d[i * SIDE : (i + 1) * SIDE, :SIDE]
        imag = d[i * SIDE : (i + 1) * SIDE, SIDE:]
        columns.append(jnp.concatenate([real * cosine - imag * sine, imag * cosine + real * sine], 0))
    high, low = split(jnp.concatenate(columns, 1))
    return dot(last[0], high) + dot(last[1], high) + dot(last[0], low)


def product(a, b):
    ar, ai, br, bi = a[:, :SIDE], a[:, SIDE:], b[:, :SIDE], b[:, SIDE:]
    return jnp.concatenate([ar * br - ai * bi, ar * bi + ai * br], 1)


def product_conj(a, b):
    ar, ai, br, bi = a[:, :SIDE], a[:, SIDE:], b[:, :SIDE], b[:, SIDE:]
    return jnp.concatenate([ar * br + ai * bi, ar * bi - ai * br], 1)


def start_exchange(me, target, source, landing, send_sem, recv_sem):
    pltpu.make_async_remote_copy(
        src_ref=source.at[target],
        dst_ref=landing.at[me],
        send_sem=send_sem.at[target],
        recv_sem=recv_sem.at[me],
        device_id={"seq": target},
        device_id_type=pl.DeviceIdType.MESH,
    ).start()


def wait_arrival(origin, source, landing, send_sem, recv_sem):
    pltpu.make_async_remote_copy(
        src_ref=source.at[origin],
        dst_ref=landing.at[origin],
        send_sem=send_sem.at[origin],
        recv_sem=recv_sem.at[origin],
        device_id={"seq": origin},
        device_id_type=pl.DeviceIdType.MESH,
    ).wait_recv()


def wait_departure(target, source, landing, send_sem, recv_sem):
    pltpu.make_async_remote_copy(
        src_ref=source.at[target],
        dst_ref=landing.at[target],
        send_sem=send_sem.at[target],
        recv_sem=recv_sem.at[target],
        device_id={"seq": target},
        device_id_type=pl.DeviceIdType.MESH,
    ).wait_send()


def stacked(upper, lower):
    return jnp.concatenate([upper, lower], 0)


def beside(left, right):
    return jnp.concatenate([left, right], 1)


def whole_kernel(
    gate, key, value, filt, rate, weight, cotangent, first, twist, forward, backward, last,
    gate_grad, key_grad, value_grad, filter_grad, weight_grad,
    send1, recv1, send2, recv2, send3, recv3, send4, recv4,
    gathered, upstream, envelope, rows1, rows2, specs, out1, out2, gated,
    partial, core_in, chip_sum, x_in, x_sum, z_in,
    ss1, rs1, ss2, rs2, ss3, rs3, ss4, rs4, ag_send, ag_recv, core_send, core_recv, x_send, x_recv, z_send, z_recv,
):
    me = lax.axis_index("seq")
    group = lax.axis_index("chan")
    owners = gate.shape[0] // OWNED
    core = me % 2
    sibling = me + 1 - 2 * core
    z = (me // 2) % 4
    x = me // 8
    far = group + 1 - 2 * (group % 2)
    pairs = owners // 2
    blocks = gate.shape[0]
    owner = me < owners
    MESH = pl.DeviceIdType.MESH

    barrier = pltpu.get_barrier_semaphore()

    @pl.loop(1, PIECES)
    def _(k):
        pl.semaphore_signal(barrier, inc=1, device_id={"seq": (me + k) % PIECES}, device_id_type=MESH)

    for k in (1, 2, 3):
        pl.semaphore_signal(barrier, inc=1, device_id={"chan": (group + 2 * k) % GROUPS}, device_id_type=MESH)
    pl.semaphore_signal(barrier, inc=1, device_id={"chan": far}, device_id_type=MESH)

    gathered[pl.ds(pl.multiple_of(blocks * group, 16), blocks), :] = cotangent[...]
    gathered[pl.ds(blocks * GROUPS, 16), :] = jnp.zeros((16, gathered.shape[1]), BF16)
    gated[pl.ds(blocks, 16), :] = jnp.zeros((16, gated.shape[1]), BF16)

    position = (me * gate.shape[1] + lax.broadcasted_iota(jnp.int32, (16, gate.shape[1]), 1)).astype(F32)

    @pl.loop(0, pairs)
    def _(p):
        r = pl.ds(pl.multiple_of(16 * p, 16), 16)
        sig = key[r, :].astype(F32) * value[r, :].astype(F32)
        speed = rate[r, :]
        window = jnp.sqrt(1.0 - jnp.exp(-2.0 * speed)) * jnp.exp(-speed * position)
        envelope[r, :] = window
        ker = filt[r, :] * window
        send1[2 * p] = stacked(sig[:8], ker[:8]).astype(BF16)
        send1[2 * p + 1] = stacked(sig[8:], ker[8:]).astype(BF16)

    pl.semaphore_wait(barrier, PIECES - 1 + 4)

    def gather_copy(index, slot, target):
        rows = gathered.at[pl.ds(pl.multiple_of(blocks * slot, 16), blocks)]
        return pltpu.make_async_remote_copy(
            src_ref=rows,
            dst_ref=rows,
            send_sem=ag_send.at[index],
            recv_sem=ag_recv.at[slot],
            device_id={"chan": target},
            device_id_type=MESH,
        )

    gather_copy(0, group, far).start()
    for k in (1, 2, 3):
        gather_copy(k, group, (group + 2 * k) % GROUPS).start()

    def to_owners(source, landing, send_sem, recv_sem):
        @pl.loop(1, PIECES)
        def _(k):
            target = (me + k) % PIECES

            @pl.when(target < owners)
            def _():
                start_exchange(me, target, source, landing, send_sem, recv_sem)

        @pl.when(owner)
        def _():
            landing[me] = source[me]

    to_owners(send1, recv1, ss1, rs1)

    gather_copy(0, far, far).wait_recv()
    for k in (1, 2, 3):
        gather_copy(3 + k, far, (group + 2 * k) % GROUPS).start()

    @pl.when(owner)
    def _():
        @pl.loop(0, PIECES)
        def _(s):
            @pl.when(s != me)
            def _():
                wait_arrival(s, send1, recv1, ss1, rs1)

            piece = recv1[s].astype(F32)
            for i in range(4):
                rows1[pl.ds(pl.multiple_of((s * 4 + i) * 16, 16), 16), :] = piece[:, i * SIDE : (i + 1) * SIDE]

        @pl.loop(0, OWNED)
        def _(c):
            sig = rows1[pl.ds(c, SIDE, stride=16), :]
            ker = rows1[pl.ds(c + 8, SIDE, stride=16), :]
            spec = forward_pair(beside(sig, ker).astype(BF16), first, twist, forward, 2)
            specs[c] = spec
            out1[pl.ds(c, SIDE, stride=8), :] = backward_pair(
                product(spec[:SIDE], spec[SIDE:]), twist, backward, last, 1
            )

        @pl.loop(0, PIECES)
        def _(k):
            s = (me + k) % PIECES
            t = [out1[pl.ds(pl.multiple_of((s * 4 + i) * 8, 8), 8), :] for i in range(4)]
            send3[s] = beside(stacked(t[0], t[2]), stacked(t[1], t[3])).astype(BF16)

            @pl.when(k > 0)
            def _():
                start_exchange(me, s, send3, recv3, ss3, rs3)

            @pl.when(k == 0)
            def _():
                recv3[me] = send3[me]

    for k in (1, 2, 3):
        near = (group + 2 * k) % GROUPS
        gather_copy(0, near, near).wait_recv()
        other = near + 1 - 2 * (near % 2)
        gather_copy(0, other, near).wait_recv()
    depth = blocks * GROUPS
    for n in range(gate.shape[1] // HALF):
        cols = pl.ds(n * HALF, HALF)
        upstream[:, cols] = dot(weight[...], gathered[pl.ds(0, depth), cols])

    @pl.loop(0, pairs)
    def _(p):
        r = pl.ds(pl.multiple_of(16 * p, 16), 16)
        g = upstream[r, :] * gate[r, :].astype(F32)
        send2[2 * p] = stacked(g[:8, :HALF], g[:8, HALF:]).astype(BF16)
        send2[2 * p + 1] = stacked(g[8:, :HALF], g[8:, HALF:]).astype(BF16)

    to_owners(send2, recv2, ss2, rs2)

    @pl.loop(0, pairs)
    def _(p):
        r = pl.ds(pl.multiple_of(16 * p, 16), 16)
        for e in range(2):
            @pl.when(2 * p + e != me)
            def _():
                wait_arrival(2 * p + e, send3, recv3, ss3, rs3)

        a = recv3[2 * p].astype(F32)
        b = recv3[2 * p + 1].astype(F32)
        conv = stacked(beside(a[:8], a[8:]), beside(b[:8], b[8:]))
        gate_grad[r, :] = (upstream[r, :] * conv).astype(BF16)
        gated[r, :] = (gate[r, :].astype(F32) * conv).astype(BF16)

    for j in range(GROUPS):
        term = lax.dot_general(
            gathered[pl.ds(blocks * j, HALF), :], gated[...], (((1,), (1,)), ((), ())), preferred_element_type=F32
        )
        for g in range(4):
            partial[g % 2, 2 * j + g // 2] = term[60 * g : 60 * g + 64]

    core_copy = pltpu.make_async_remote_copy(
        src_ref=partial.at[1 - core],
        dst_ref=core_in,
        send_sem=core_send,
        recv_sem=core_recv,
        device_id={"seq": sibling},
        device_id_type=MESH,
    )
    core_copy.start()

    @pl.when(owner)
    def _():
        @pl.loop(0, PIECES)
        def _(s):
            @pl.when(s != me)
            def _():
                wait_arrival(s, send2, recv2, ss2, rs2)

            piece = recv2[s].astype(F32)
            for i in range(4):
                h, l = i // 2, i % 2
                rows2[pl.ds(pl.multiple_of((s * 4 + i) * 8, 8), 8), :] = piece[
                    h * 8 : h * 8 + 8, l * SIDE : (l + 1) * SIDE
                ]

    core_copy.wait_recv()
    chip_sum[...] = partial[core] + core_in[...]

    def x_copy(k):
        there = (x + k) % 4
        return pltpu.make_async_remote_copy(
            src_ref=chip_sum.at[pl.ds(4 * there, 4)],
            dst_ref=x_in.at[k - 1],
            send_sem=x_send.at[k - 1],
            recv_sem=x_recv.at[k - 1],
            device_id={"seq": (me + 8 * k) % PIECES},
            device_id_type=MESH,
        )

    for k in (1, 2, 3):
        x_copy(k).start()

    @pl.when(owner)
    def _():
        @pl.loop(0, OWNED)
        def _(c):
            g = rows2[pl.ds(c, SIDE, stride=8), :].astype(BF16)
            gspec = forward_pair(g, first, twist, forward, 1)
            spec = specs[c]
            both = stacked(product_conj(spec[SIDE:], gspec), product_conj(spec[:SIDE], gspec))
            y = backward_pair(both, twist, backward, last, 2)
            out2[pl.ds(c, SIDE, stride=16), :] = y[:, :SIDE]
            out2[pl.ds(c + 8, SIDE, stride=16), :] = y[:, SIDE:]

        @pl.loop(0, PIECES)
        def _(k):
            s = (me + k) % PIECES
            t = [out2[pl.ds(pl.multiple_of((s * 4 + i) * 16, 16), 16), :] for i in range(4)]
            send4[s] = jnp.concatenate(t, 1).astype(BF16)

            @pl.when(k > 0)
            def _():
                start_exchange(me, s, send4, recv4, ss4, rs4)

            @pl.when(k == 0)
            def _():
                recv4[me] = send4[me]

    for k in (1, 2, 3):
        x_copy(k).wait_recv()
    x_sum[...] = chip_sum[pl.ds(4 * x, 4)] + x_in[0] + x_in[1] + x_in[2]

    def z_copy(k):
        there = (z + k) % 4
        return pltpu.make_async_remote_copy(
            src_ref=x_sum.at[there],
            dst_ref=z_in.at[k - 1],
            send_sem=z_send.at[k - 1],
            recv_sem=z_recv.at[k - 1],
            device_id={"seq": x * 8 + there * 2 + core},
            device_id_type=MESH,
        )

    for k in (1, 2, 3):
        z_copy(k).start()

    @pl.loop(0, pairs)
    def _(p):
        r = pl.ds(pl.multiple_of(16 * p, 16), 16)
        for e in range(2):
            @pl.when(2 * p + e != me)
            def _():
                wait_arrival(2 * p + e, send4, recv4, ss4, rs4)

        a = recv4[2 * p].astype(F32)
        b = recv4[2 * p + 1].astype(F32)
        sgrad = stacked(a[:8], b[:8])
        kgrad = stacked(a[8:], b[8:])
        key_grad[r, :] = (sgrad * value[r, :].astype(F32)).astype(BF16)
        value_grad[r, :] = (sgrad * key[r, :].astype(F32)).astype(BF16)
        filter_grad[r, :] = kgrad * envelope[r, :]

    for k in (1, 2, 3):
        z_copy(k).wait_recv()
    total = x_sum[z] + z_in[0] + z_in[1] + z_in[2]
    turned = stacked(total, total).T
    weight_grad[...] = turned[:blocks, : weight_grad.shape[1]]

    for k in (1, 2, 3):
        x_copy(k).wait_send()
        z_copy(k).wait_send()
        gather_copy(k, group, (group + 2 * k) % GROUPS).wait_send()
        gather_copy(3 + k, far, (group + 2 * k) % GROUPS).wait_send()
    gather_copy(0, group, far).wait_send()
    core_copy.wait_send()

    @pl.loop(1, PIECES)
    def _(k):
        target = (me + k) % PIECES

        @pl.when(target < owners)
        def _():
            wait_departure(target, send1, recv1, ss1, rs1)
            wait_departure(target, send2, recv2, ss2, rs2)

        @pl.when(owner)
        def _():
            wait_departure(target, send3, recv3, ss3, rs3)
            wait_departure(target, send4, recv4, ss4, rs4)


def per_device(gate_act, key_act, value_act, filter_raw, decay_rate, out_weight, out_grad):
    channels, length = gate_act.shape
    tables = [jnp.asarray(t) for t in make_tables()]
    shape = (channels, length)
    vmem = pltpu.VMEM
    dma = pltpu.SemaphoreType.DMA
    rows = SIDE * OWNED
    return pl.pallas_call(
        whole_kernel,
        out_shape=(
            jax.ShapeDtypeStruct(shape, BF16),
            jax.ShapeDtypeStruct(shape, BF16),
            jax.ShapeDtypeStruct(shape, BF16),
            jax.ShapeDtypeStruct(shape, F32),
            jax.ShapeDtypeStruct((channels, channels * GROUPS // PIECES), F32),
        ),
        scratch_shapes=[
            vmem((PIECES, 16, length), BF16),
            vmem((PIECES, 16, length), BF16),
            vmem((PIECES, 16, HALF), BF16),
            vmem((PIECES, 16, HALF), BF16),
            vmem((PIECES, 16, HALF), BF16),
            vmem((PIECES, 16, HALF), BF16),
            vmem((PIECES, 16, length), BF16),
            vmem((PIECES, 16, length), BF16),
            vmem((channels * GROUPS + 16, length), BF16),
            vmem(shape, F32),
            vmem(shape, F32),
            vmem((2 * rows, SIDE), F32),
            vmem((rows, SIDE), F32),
            vmem((OWNED, 2 * SIDE, 2 * SIDE), F32),
            vmem((rows, SIDE), F32),
            vmem((2 * rows, SIDE), F32),
            vmem((channels + 16, length), BF16),
            vmem((2, 16, 64, HALF), F32),
            vmem((16, 64, HALF), F32),
            vmem((16, 64, HALF), F32),
            vmem((3, 4, 64, HALF), F32),
            vmem((4, 64, HALF), F32),
            vmem((3, 64, HALF), F32),
        ]
        + [dma((PIECES,))] * 8
        + [dma((7,)), dma((GROUPS,)), dma, dma, dma((3,)), dma((3,)), dma((3,)), dma((3,))],
        compiler_params=pltpu.CompilerParams(
            collective_id=0, has_side_effects=True, vmem_limit_bytes=50 * 2**20
        ),
    )(gate_act, key_act, value_act, filter_raw, decay_rate[:, None], out_weight, out_grad, *tables)


def solution(mesh):
    rows = P("chan", "seq")
    return jax.shard_map(
        per_device,
        mesh=mesh,
        in_specs=(rows, rows, rows, rows, P("chan"), P("chan", None), rows),
        out_specs=(rows,) * 5,
        check_vma=False,
    )
```

time: 290 us -> 96.9 us (0.33)
  waiting for transfers between devices: 207 us -> 0 us
  Pallas kernels: 11.6 us -> 82.8 us
  starting transfers between devices: 25.3 us -> 0 us
  blocking collectives: 14.7 us -> 0 us
  between operations: 14.3 us -> 0.67 us
  local copies, waits for them, and re-layouts: 7.15 us -> 13 us
  matrix products: 5.42 us -> 0 us
  other arithmetic: 4.55 us -> 0 us
    reduce_scatter x1 -> x0, waiting for transfers between devices: 112 us -> none  [per_device(): lax.psum_scatter(partial, 'seq', scatter_dimension=0, tiled=False)]
    pallas_call x1, Pallas kernels: 11.6 us -> 82.8 us  [per_device(): pl.pallas_call(whole_kernel, out_shape=(jax.ShapeDtypeStruct(shape, BF16)...]
    all_gather x1 -> x0, waiting for transfers between devices: 52 us -> none  [per_device(): everything = lax.all_gather(out_grad, 'chan', axis=0, tiled=True)]
    all_to_all x5 -> x0, waiting for transfers between devices: 41.8 us -> none  [the longest x3 21 us: gather_rows(): lax.all_to_all(x.reshape(pieces, OWNED, length), 'seq', split_axis=0, con...]
    all_to_all x5 -> x0, starting transfers between devices: 25.2 us -> none  [the longest x3 17.3 us: gather_rows(): lax.all_to_all(x.reshape(pieces, OWNED, length), 'seq', split_axis=0, con...]
    all_to_all x1 -> x0, blocking collectives: 14.7 us -> none  [scatter_rows(): x = lax.all_to_all(x, 'seq', split_axis=0, concat_axis=0, tiled=True)]
    unnamed x28 -> x24, local copies, waits for them, and re-layouts: 0.79 us -> 11.4 us
    reshape x16 -> x0, local copies, waits for them, and re-layouts: 6.36 us -> none  [the longest x3 2.18 us: gather_rows(): x.reshape(pieces, OWNED, length)]
  transfers between devices with their start and end apart: 7 -> 0, of which waited for: 6 -> 0; matrix products, arithmetic and copies ran while one was open for 4% -> 0% of each run, Pallas kernels for 0% -> 0%
where the time goes in v2:
time: 96.9 us; the launch traced here: 96.5 us
  Pallas kernels  82.8 us (85%)
  local copies, waits for them, and re-layouts  13 us (13%)
    pallas_call x1, Pallas kernels, per_device(): pl.pallas_call(whole_kernel, out_shape=(jax.ShapeDtypeStruct(shape, BF16)...  82.8 us
    unnamed x24, local copies, waits for them, and re-layouts  11.4 us

profile of v2, /device:TPU:16, one launch (start us, length us, event | category | flops | bytes accessed | tf_op | source)
XLA Modules:
  0.0 96.5 jit_solution(4068434121383920923)
XLA Ops:
  0.6 0.0 copy-start.7
  0.6 0.8 copy.18.rate
  1.5 0.1 copy-done.7
  1.6 0.0 copy-start
  1.6 1.0 %copy-done = f32[240,512]{1,0:T(8,128)S(1)} copy-done((f32[240,512]{1,0:T(8,128)S(1)}, f32[240,512]{1,0:T(8,128)}, u32[]{:S(2)}) %copy-start) | copy-done | bytes 491544
  2.6 0.0 copy-start.1
  2.6 0.9 copy-done.1
  3.5 0.0 copy-start.2
  3.5 0.9 copy-done.2
  4.5 0.0 copy-start.3
  4.5 0.9 copy-done.3
  5.4 0.0 copy-start.4
  5.4 0.9 copy-done.4
  6.4 0.0 copy-start.5
  6.4 0.9 copy-done.5
  7.3 0.0 copy-start.6
  7.3 0.9 copy-done.6
  8.3 0.0 copy-start.8
  8.3 0.9 copy-done.8
  9.2 0.0 copy-start.9
  9.2 0.9 copy-done.9
  10.1 82.8 %shard_map.155 = (bf16[240,512]{1,0:T(8,128)(2,1)S(1)}, bf16[240,512]{1,0:T(8,128)(2,1)S(1)}, bf16[240,512]{1,0:T(8,128)(2,1)S(1)}, f32[240,512]{1,0:T(8,128)S(1)}, f32[240,60]{1,0:T(8,128)S(1)}) custom-call(bf16[240,512]{1,0:T(8,128)(2,1)S(1)} %copy-done.3, bf16[240,512]{1,0:T(8,128)(2,1)S(1)} %copy-done.4, bf16[240,512]{1,0:T(8,128)(2,1)S(1)} %copy-done.5, ...), custom_call_target="tpu_custom_call" | custom-call | tf_op jit(solution)/shard_map/pallas_call | solution.py:433
  92.9 0.7 copy.19
  93.6 0.7 copy.24
  94.3 0.7 copy.25
  95.0 0.7 copy.26
  95.7 0.8 copy.27
Async XLA Ops:
  0.6 0.9 copy-start.7
  1.6 1.0 %copy-start = (f32[240,512]{1,0:T(8,128)S(1)}, f32[240,512]{1,0:T(8,128)}, u32[]{:S(2)}) copy-start(f32[240,512]{1,0:T(8,128)} %filt.1) | copy-start | bytes 1474564
  2.6 0.9 copy-start.1
  3.5 0.9 copy-start.2
  4.5 0.9 copy-start.3
  5.4 0.9 copy-start.4
  6.4 0.9 copy-start.5
  7.3 0.9 copy-start.6
  8.3 0.9 copy-start.8
  9.2 0.9 copy-start.9

commit v3 on v2

v3 whole, which is shorter than its diff:
```python
import functools
import math

import jax
import jax.numpy as jnp
import numpy as np
from jax import lax
from jax.experimental import pallas as pl
from jax.experimental.pallas import tpu as pltpu
from jax.sharding import PartitionSpec as P

F32 = jnp.float32
BF16 = jnp.bfloat16
SIDE = 128
LENGTH = SIDE * SIDE
OWNED = 8
PIECES = 32
GROUPS = 8
HALF = 256
BATCH = 4
LIMIT = 63 * 2**20
CHUNKS = ((0, 64), (64, 64), (128, 64), (192, 48))
MESH = pl.DeviceIdType.MESH


def halves(table):
    high = np.asarray(table, np.float32).astype(jnp.bfloat16)
    low = (np.asarray(table, np.float64) - high.astype(np.float64)).astype(np.float32).astype(jnp.bfloat16)
    return high, low


def make_tables():
    n = np.arange(SIDE, dtype=np.float64)
    outer = 2.0 * np.pi * np.outer(n + 0.25, n) / SIDE
    first = np.concatenate([np.cos(outer), -np.sin(outer)], 0)
    first_high, first_low = halves(first)
    first_both = np.concatenate([first_high, first_low], 1)
    turn = 2.0 * np.pi * np.outer(n + 0.25, n) / LENGTH
    twist = np.stack([np.cos(turn), np.sin(turn)]).astype(np.float32)
    inner = 2.0 * np.pi * np.outer(n, n) / SIDE
    cosine, sine = np.cos(inner), np.sin(inner)
    forward = np.concatenate([np.concatenate([cosine, -sine], 1), np.concatenate([sine, cosine], 1)], 0)
    backward = np.concatenate([np.concatenate([cosine, sine], 1), np.concatenate([-sine, cosine], 1)], 0)
    last = np.concatenate([np.cos(outer.T), -np.sin(outer.T)], 1) / LENGTH
    return (
        first_both.astype(np.float32),
        twist,
        np.stack(halves(forward)).astype(np.float32),
        np.stack(halves(backward)).astype(np.float32),
        np.stack(halves(last)).astype(np.float32),
    )


def dot(a, b):
    return jnp.dot(a, b, preferred_element_type=F32)


def split(x):
    high = x.astype(BF16)
    return high, (x - high.astype(F32)).astype(BF16)


def forward_pair(x, first, twist, forward, count):
    a = dot(first[...], jnp.concatenate([x, x], 0))
    cosine, sine = twist[0], twist[1]
    rows = []
    for i in range(count):
        real = a[:SIDE, i * SIDE : (i + 1) * SIDE]
        imag = a[SIDE:, i * SIDE : (i + 1) * SIDE]
        rows.append(jnp.concatenate([real * cosine + imag * sine, imag * cosine - real * sine], 1))
    high, low = split(jnp.concatenate(rows, 0))
    return dot(jnp.concatenate([high, high, low], 1), forward[...])


def backward_pair(spec, twist, backward, last, count):
    high, low = split(spec)
    d = dot(jnp.concatenate([high, high, low], 1), backward[...])
    cosine, sine = twist[0], twist[1]
    columns = []
    for i in range(count):
        real = d[i * SIDE : (i + 1) * SIDE, :SIDE]
        imag = d[i * SIDE : (i + 1) * SIDE, SIDE:]
        columns.append(jnp.concatenate([real * cosine - imag * sine, imag * cosine + real * sine], 0))
    high, low = split(jnp.concatenate(columns, 1))
    return dot(last[...], jnp.concatenate([high, high, low], 0))


def product(a, b):
    ar, ai, br, bi = a[:, :SIDE], a[:, SIDE:], b[:, :SIDE], b[:, SIDE:]
    return jnp.concatenate([ar * br - ai * bi, ar * bi + ai * br], 1)


def product_conj(a, b):
    ar, ai, br, bi = a[:, :SIDE], a[:, SIDE:], b[:, :SIDE], b[:, SIDE:]
    return jnp.concatenate([ar * br + ai * bi, ar * bi - ai * br], 1)


def go(copy):
    copy.start()


def land(copy):
    copy.wait_recv()


def leave(copy):
    copy.wait_send()


def exchange(me, target, source, landing, send_sem, recv_sem):
    return pltpu.make_async_remote_copy(
        src_ref=source.at[target],
        dst_ref=landing.at[me],
        send_sem=send_sem.at[target],
        recv_sem=recv_sem.at[me],
        device_id={"seq": target},
        device_id_type=MESH,
    )


def arrival(origin, source, landing, send_sem, recv_sem):
    return exchange(origin, origin, source, landing, send_sem, recv_sem)


def stacked(upper, lower):
    return jnp.concatenate([upper, lower], 0)


def beside(left, right):
    return jnp.concatenate([left, right], 1)


def whole_kernel(
    gate_hbm, key_hbm, value_hbm, filt_hbm, rate_hbm, weight_hbm, cotangent_hbm,
    first_hbm, twist_hbm, forward_hbm, backward_hbm, last_hbm,
    gate_grad, key_grad, value_grad, filter_grad, weight_grad,
    gate, key, value, filt, rate, weight, first_in, twist, forward_in, backward_in, last_in,
    first, forward, backward, last,
    send1, recv1, send2, recv2, send3, recv3, send4, recv4,
    gathered, upstream, envelope, rows1, rows2, specs, out1, out2, gated,
    partial, core_in, chip_sum, x_in, x_sum, z_in, in_sem,
    ss1, rs1, ss2, rs2, ss3, rs3, ss4, rs4, ag_send, ag_recv, core_send, core_recv, x_send, x_recv, z_send, z_recv,
):
    me = lax.axis_index("seq")
    group = lax.axis_index("chan")
    blocks = gate.shape[0]
    length = gate.shape[1]
    owners = blocks // OWNED
    core = me % 2
    sibling = me + 1 - 2 * core
    z = (me // 2) % 4
    x = me // 8
    far = group + 1 - 2 * (group % 2)
    above = (group + 2) % GROUPS
    below = (group + GROUPS - 2) % GROUPS
    pairs = owners // 2
    owner = me < owners
    own_rows = pl.ds(pl.multiple_of(blocks * group, 16), blocks)

    loads = [
        pltpu.make_async_copy(a, b, in_sem.at[i])
        for i, (a, b) in enumerate(
            (
                (key_hbm, key),
                (value_hbm, value),
                (filt_hbm, filt),
                (rate_hbm, rate),
                (cotangent_hbm, gathered.at[own_rows]),
                (gate_hbm, gate),
                (first_hbm, first_in),
                (twist_hbm, twist),
                (forward_hbm, forward_in),
                (backward_hbm, backward_in),
                (last_hbm, last_in),
                (weight_hbm, weight),
            )
        )
    ]
    for load in loads:
        load.start()
    barrier = pltpu.get_barrier_semaphore()

    @pl.loop(1, PIECES)
    def _(k):
        pl.semaphore_signal(barrier, inc=1, device_id={"seq": (me + k) % PIECES}, device_id_type=MESH)

    for peer in (far, above, below):
        pl.semaphore_signal(barrier, inc=1, device_id={"chan": peer}, device_id_type=MESH)

    gathered[pl.ds(blocks * GROUPS, 16), :] = jnp.zeros((16, length), BF16)
    gated[pl.ds(blocks, 16), :] = jnp.zeros((16, 2 * length), BF16)
    position = (me * length + lax.broadcasted_iota(jnp.int32, (16, length), 1)).astype(F32)
    for load in loads[:4]:
        load.wait()

    @pl.loop(0, pairs)
    def _(p):
        r = pl.ds(pl.multiple_of(16 * p, 16), 16)
        sig = key[r, :].astype(F32) * value[r, :].astype(F32)
        speed = rate[r, :]
        window = jnp.sqrt(1.0 - jnp.exp(-2.0 * speed)) * jnp.exp(-speed * position)
        envelope[r, :] = window
        ker = filt[r, :] * window
        send1[2 * p] = stacked(sig[:8], ker[:8]).astype(BF16)
        send1[2 * p + 1] = stacked(sig[8:], ker[8:]).astype(BF16)

    loads[4].wait()
    pl.semaphore_wait(barrier, PIECES - 1 + 3)

    def gather_copy(index, slot, chunk, target):
        begin, count = CHUNKS[chunk]
        rows = gathered.at[pl.ds(pl.multiple_of(blocks * slot + begin, 16), count)]
        return pltpu.make_async_remote_copy(
            src_ref=rows,
            dst_ref=rows,
            send_sem=ag_send.at[index, chunk],
            recv_sem=ag_recv.at[slot, chunk],
            device_id={"chan": target},
            device_id_type=MESH,
        )

    span = range(len(CHUNKS))
    middle = len(CHUNKS) // 2
    above_far = above + 1 - 2 * (above % 2)
    below_far = below + 1 - 2 * (below % 2)

    def relay(index, from_below, from_above, chunk):
        if chunk < middle:
            return gather_copy(index, from_below, chunk, above)
        return gather_copy(index, from_above, chunk, below)

    def to_owners(source, landing, send_sem, recv_sem):
        @pl.loop(1, PIECES)
        def _(k):
            target = (me + k) % PIECES

            @pl.when(target < owners)
            def _():
                go(exchange(me, target, source, landing, send_sem, recv_sem))

        @pl.when(owner)
        def _():
            landing[me] = source[me]

    def pass_far(c):
        land(gather_copy(0, far, c, far))
        go(gather_copy(3, far, c, above))
        go(gather_copy(4, far, c, below))

    go(gather_copy(0, group, 0, far))
    go(gather_copy(0, group, 1, far))
    for c in span:
        go(gather_copy(1, group, c, above))
        go(gather_copy(2, group, (c + middle) % len(CHUNKS), below))
    for load in loads[5:]:
        load.wait()
    first[...] = first_in[...].astype(BF16)
    for i, part in enumerate((0, 1, 0)):
        rows = pl.ds(2 * SIDE * i, 2 * SIDE)
        forward[rows, :] = forward_in[part].astype(BF16)
        backward[rows, :] = backward_in[part].astype(BF16)
        last[:, rows] = last_in[part].astype(BF16)
    pass_far(0)
    go(gather_copy(0, group, 2, far))
    pass_far(1)
    go(gather_copy(0, group, 3, far))
    to_owners(send1, recv1, ss1, rs1)
    for c in span:
        land(relay(5, below, above, c))
        go(relay(5, below, above, c))
    pass_far(2)
    pass_far(3)
    for c in span:
        land(relay(6, below_far, above_far, c))
        go(relay(6, below_far, above_far, c))

    for c in span:
        if c < middle:
            land(gather_copy(0, above, c, above))
            land(gather_copy(0, above_far, c, above))
        else:
            land(gather_copy(0, below, c, below))
            land(gather_copy(0, below_far, c, below))
        opposite = (group + 4) % GROUPS
        land(gather_copy(0, opposite, c, above))
        land(gather_copy(0, opposite + 1 - 2 * (opposite % 2), c, above))
    depth = blocks * GROUPS
    for n in range(length // HALF):
        cols = pl.ds(n * HALF, HALF)
        upstream[:, cols] = dot(weight[...], gathered[pl.ds(0, depth), cols])

    @pl.loop(0, pairs)
    def _(p):
        r = pl.ds(pl.multiple_of(16 * p, 16), 16)
        g = upstream[r, :] * gate[r, :].astype(F32)
        send2[2 * p] = stacked(g[:8, :HALF], g[:8, HALF:]).astype(BF16)
        send2[2 * p + 1] = stacked(g[8:, :HALF], g[8:, HALF:]).astype(BF16)

    to_owners(send2, recv2, ss2, rs2)

    @pl.when(owner)
    def _():
        @pl.loop(0, PIECES)
        def _(s):
            @pl.when(s != me)
            def _():
                land(arrival(s, send1, recv1, ss1, rs1))

        @pl.loop(0, PIECES, unroll=4)
        def _(s):
            piece = recv1[s].astype(F32)
            for i in range(4):
                rows1[pl.ds(pl.multiple_of((s * 4 + i) * 16, 16), 16), :] = piece[:, i * SIDE : (i + 1) * SIDE]

        @pl.loop(0, OWNED // BATCH)
        def _(b):
            cs = [b * BATCH + i for i in range(BATCH)]
            sig = [rows1[pl.ds(c, SIDE, stride=16), :].astype(BF16) for c in cs]
            ker = [rows1[pl.ds(c + 8, SIDE, stride=16), :].astype(BF16) for c in cs]
            spec = forward_pair(jnp.concatenate(sig + ker, 1), first, twist, forward, 2 * BATCH)
            specs[b] = spec
            y = backward_pair(
                product(spec[: SIDE * BATCH], spec[SIDE * BATCH :]), twist, backward, last, BATCH
            )
            for i, c in enumerate(cs):
                out1[pl.ds(c, SIDE, stride=8), :] = y[:, i * SIDE : (i + 1) * SIDE]

        @pl.loop(0, PIECES, unroll=4)
        def _(s):
            t = [out1[pl.ds(pl.multiple_of((s * 4 + i) * 8, 8), 8), :] for i in range(4)]
            send3[s] = beside(stacked(t[0], t[2]), stacked(t[1], t[3])).astype(BF16)

        @pl.loop(1, PIECES)
        def _(k):
            go(exchange(me, (me + k) % PIECES, send3, recv3, ss3, rs3))

        recv3[me] = send3[me]

    @pl.when(owner)
    def _():
        @pl.loop(0, PIECES)
        def _(s):
            @pl.when(s != me)
            def _():
                land(arrival(s, send2, recv2, ss2, rs2))

        @pl.loop(0, PIECES, unroll=4)
        def _(s):
            piece = recv2[s].astype(F32)
            for i in range(4):
                h, l = i // 2, i % 2
                rows2[pl.ds(pl.multiple_of((s * 4 + i) * 8, 8), 8), :] = piece[
                    h * 8 : h * 8 + 8, l * SIDE : (l + 1) * SIDE
                ]

        @pl.loop(0, OWNED // BATCH)
        def _(b):
            cs = [b * BATCH + i for i in range(BATCH)]
            g = [rows2[pl.ds(c, SIDE, stride=8), :].astype(BF16) for c in cs]
            gspec = forward_pair(jnp.concatenate(g, 1), first, twist, forward, BATCH)
            spec = specs[b]
            both = stacked(
                product_conj(spec[SIDE * BATCH :], gspec), product_conj(spec[: SIDE * BATCH], gspec)
            )
            y = backward_pair(both, twist, backward, last, 2 * BATCH)
            for i in range(2 * BATCH):
                out2[pl.ds(i, SIDE, stride=8), :] = y[:, i * SIDE : (i + 1) * SIDE]

            @pl.loop(0, PIECES, unroll=4)
            def _(s):
                t = [out2[pl.ds(pl.multiple_of((s * 4 + i) * 8, 8), 8), :] for i in range(4)]
                send4[b, s] = beside(stacked(t[0], t[2]), stacked(t[1], t[3])).astype(BF16)

            @pl.loop(1, PIECES)
            def _(k):
                go(exchange(me, (me + k) % PIECES, send4.at[b], recv4.at[b], ss4.at[b], rs4.at[b]))

            recv4[b, me] = send4[b, me]

    def from_owners(source, landing, send_sem, recv_sem):
        @pl.loop(0, owners)
        def _(s):
            @pl.when(s != me)
            def _():
                land(arrival(s, source, landing, send_sem, recv_sem))

    from_owners(send3, recv3, ss3, rs3)

    @pl.loop(0, pairs)
    def _(p):
        r = pl.ds(pl.multiple_of(16 * p, 16), 16)
        a = recv3[2 * p].astype(F32)
        b = recv3[2 * p + 1].astype(F32)
        conv = stacked(beside(a[:8], a[8:]), beside(b[:8], b[8:]))
        gate_grad[r, :] = (upstream[r, :] * conv).astype(BF16)
        high, low = split(gate[r, :].astype(F32) * conv)
        gated[r, :] = beside(high, low)

    for j in range(GROUPS):
        rows = gathered[pl.ds(blocks * j, HALF), :]
        term = lax.dot_general(
            beside(rows, rows), gated[...], (((1,), (1,)), ((), ())), preferred_element_type=F32
        )
        for g in range(4):
            partial[g % 2, 2 * j + g // 2] = term[60 * g : 60 * g + 64]

    core_copy = pltpu.make_async_remote_copy(
        src_ref=partial.at[1 - core],
        dst_ref=core_in,
        send_sem=core_send,
        recv_sem=core_recv,
        device_id={"seq": sibling},
        device_id_type=MESH,
    )
    go(core_copy)

    def x_copy(k):
        there = (x + k) % 4
        return pltpu.make_async_remote_copy(
            src_ref=chip_sum.at[pl.ds(4 * there, 4)],
            dst_ref=x_in.at[k - 1],
            send_sem=x_send.at[k - 1],
            recv_sem=x_recv.at[k - 1],
            device_id={"seq": (me + 8 * k) % PIECES},
            device_id_type=MESH,
        )

    land(core_copy)
    partial[core] = partial[core] + core_in[...]
    chip_sum[...] = partial[core].astype(BF16)
    for k in (1, 2, 3):
        go(x_copy(k))

    for k in (1, 2, 3):
        land(x_copy(k))
    x_sum[...] = partial[core, pl.ds(4 * x, 4)] + x_in[0].astype(F32) + x_in[1].astype(F32) + x_in[2].astype(F32)

    def z_copy(k):
        there = (z + k) % 4
        return pltpu.make_async_remote_copy(
            src_ref=x_sum.at[there],
            dst_ref=z_in.at[k - 1],
            send_sem=z_send.at[k - 1],
            recv_sem=z_recv.at[k - 1],
            device_id={"seq": x * 8 + there * 2 + core},
            device_id_type=MESH,
        )

    for k in (1, 2, 3):
        go(z_copy(k))

    for b in range(2):
        from_owners(send4.at[b], recv4.at[b], ss4.at[b], rs4.at[b])

    @pl.loop(0, pairs)
    def _(p):
        r = pl.ds(pl.multiple_of(16 * p, 16), 16)
        parts = []
        for o in range(2):
            for b in range(2):
                a = recv4[b, 2 * p + o].astype(F32)
                parts.append(beside(a[:8], a[8:]))
        sgrad = jnp.concatenate([a[:4] for a in parts], 0)
        kgrad = jnp.concatenate([a[4:] for a in parts], 0)
        key_grad[r, :] = (sgrad * value[r, :].astype(F32)).astype(BF16)
        value_grad[r, :] = (sgrad * key[r, :].astype(F32)).astype(BF16)
        filter_grad[r, :] = kgrad * envelope[r, :]

    for k in (1, 2, 3):
        land(z_copy(k))
    total = x_sum[z] + z_in[0] + z_in[1] + z_in[2]
    weight_grad[...] = total[: weight_grad.shape[0], :blocks]

    for k in (1, 2, 3):
        leave(x_copy(k))
        leave(z_copy(k))
    leave(core_copy)
    for c in span:
        leave(gather_copy(0, group, c, far))
        leave(gather_copy(1, group, c, above))
        leave(gather_copy(2, group, c, below))
        leave(gather_copy(3, far, c, above))
        leave(gather_copy(4, far, c, below))
        leave(relay(5, below, above, c))
        leave(relay(6, below_far, above_far, c))

    @pl.loop(1, PIECES)
    def _(k):
        target = (me + k) % PIECES

        @pl.when(target < owners)
        def _():
            leave(exchange(me, target, send1, recv1, ss1, rs1))
            leave(exchange(me, target, send2, recv2, ss2, rs2))

        @pl.when(owner)
        def _():
            leave(exchange(me, target, send3, recv3, ss3, rs3))
            for b in range(2):
                leave(exchange(me, target, send4.at[b], recv4.at[b], ss4.at[b], rs4.at[b]))


def per_device(gate_act, key_act, value_act, filter_raw, decay_rate, out_weight, out_grad):
    channels, length = gate_act.shape
    tables = [jnp.asarray(t) for t in make_tables()]
    shape = (channels, length)
    vmem = pltpu.VMEM
    dma = pltpu.SemaphoreType.DMA
    rows = SIDE * OWNED
    *grads, weight_grad = pl.pallas_call(
        whole_kernel,
        out_shape=(
            jax.ShapeDtypeStruct(shape, BF16),
            jax.ShapeDtypeStruct(shape, BF16),
            jax.ShapeDtypeStruct(shape, BF16),
            jax.ShapeDtypeStruct(shape, F32),
            jax.ShapeDtypeStruct((channels * GROUPS // PIECES, channels), F32),
        ),
        in_specs=[pl.BlockSpec(memory_space=pltpu.HBM)] * 12,
        scratch_shapes=[
            vmem(shape, BF16),
            vmem(shape, BF16),
            vmem(shape, BF16),
            vmem(shape, F32),
            vmem((channels, 1), F32),
            vmem(out_weight.shape, BF16),
        ]
        + [vmem(t.shape, t.dtype) for t in tables]
        + [
            vmem((2 * SIDE, 2 * SIDE), BF16),
            vmem((6 * SIDE, 2 * SIDE), BF16),
            vmem((6 * SIDE, 2 * SIDE), BF16),
            vmem((SIDE, 6 * SIDE), BF16),
            vmem((PIECES, 16, length), BF16),
            vmem((PIECES, 16, length), BF16),
            vmem((PIECES, 16, HALF), BF16),
            vmem((PIECES, 16, HALF), BF16),
            vmem((PIECES, 16, HALF), BF16),
            vmem((PIECES, 16, HALF), BF16),
            vmem((2, PIECES, 16, HALF), BF16),
            vmem((2, PIECES, 16, HALF), BF16),
            vmem((channels * GROUPS + 16, length), BF16),
            vmem(shape, F32),
            vmem(shape, F32),
            vmem((2 * rows, SIDE), F32),
            vmem((rows, SIDE), F32),
            vmem((OWNED // BATCH, 2 * SIDE * BATCH, 2 * SIDE), F32),
            vmem((rows, SIDE), F32),
            vmem((rows, SIDE), F32),
            vmem((channels + 16, 2 * length), BF16),
            vmem((2, 16, 64, HALF), F32),
            vmem((16, 64, HALF), F32),
            vmem((16, 64, HALF), BF16),
            vmem((3, 4, 64, HALF), BF16),
            vmem((4, 64, HALF), F32),
            vmem((3, 64, HALF), F32),
            dma((12,)),
        ]
        + [dma((PIECES,))] * 6
        + [dma((2, PIECES))] * 2
        + [dma((7, len(CHUNKS))), dma((GROUPS, len(CHUNKS))), dma, dma]
        + [dma((3,))] * 4,
        compiler_params=pltpu.CompilerParams(
            collective_id=0, has_side_effects=True, vmem_limit_bytes=LIMIT
        ),
    )(gate_act, key_act, value_act, filter_raw, decay_rate[:, None], out_weight, out_grad, *tables)
    return (*grads, weight_grad.T)


def solution(mesh):
    rows = P("chan", "seq")
    return jax.shard_map(
        per_device,
        mesh=mesh,
        in_specs=(rows, rows, rows, rows, P("chan"), P("chan", None), rows),
        out_specs=(rows,) * 5,
        check_vma=False,
    )
```

time: 96.9 us -> 83.2 us (0.86)
  local copies, waits for them, and re-layouts: 13 us -> 6.06 us
  Pallas kernels: 82.8 us -> 76.3 us
    pallas_call x1, Pallas kernels: 82.8 us -> 76.3 us  [per_device(): pl.pallas_call(whole_kernel, out_shape=(jax.ShapeDtypeStruct(shape, BF16)...]
    unnamed x24 -> x15, local copies, waits for them, and re-layouts: 11.4 us -> 5.27 us
where the time goes in v3:
time: 83.2 us; the launch traced here: 83.1 us
  Pallas kernels  76.3 us (92%)
  local copies, waits for them, and re-layouts  6.06 us (7%)
    pallas_call x1, Pallas kernels, per_device(): pl.pallas_call(whole_kernel, out_shape=(jax.ShapeDtypeStruct(shape, BF16)...  76.3 us
    unnamed x15, local copies, waits for them, and re-layouts  5.27 us

profile of v3, /device:TPU:16, one launch (start us, length us, event | category | flops | bytes accessed | tf_op | source)
XLA Modules:
  0.0 83.1 jit_solution(7453647489666217330)
XLA Ops:
  0.6 0.0 copy-start.4
  0.6 0.7 copy-done.4
  1.3 0.8 copy.17.rate_hbm
  2.1 76.3 %shard_map.155 = (bf16[240,512]{1,0:T(8,128)(2,1)}, bf16[240,512]{1,0:T(8,128)(2,1)}, bf16[240,512]{1,0:T(8,128)(2,1)}, f32[240,512]{1,0:T(8,128)}, f32[60,240]{1,0:T(8,128)}) custom-call(bf16[240,512]{1,0:T(8,128)(2,1)} %gate_hbm.1, bf16[240,512]{1,0:T(8,128)(2,1)} %key_hbm.1, bf16[240,512]{1,0:T(8,128)(2,1)} %value_hbm.1, f32[240,512]{1,0:T(8,128)} %filt_hbm.1, ...), custom_call_target="tpu_custom_call" | custom-call | tf_op jit(solution)/shard_map/pallas_call | solution.py:510
  78.5 0.0 copy-start.2
  78.5 0.0 copy-start.1
  78.5 1.7 %copy.23 = bf16[240,512]{1,0:T(8,128)(2,1)} copy(bf16[240,512]{1,0:T(8,128)(2,1)} %get-tuple-element.20) | data formatting | bytes 491520
  80.2 0.0 copy-done.2
  80.2 0.0 copy-start
  80.2 0.7 copy.24
  80.9 0.0 copy-done.1
  80.9 0.7 copy.25
  81.6 0.0 copy-done
  81.6 0.0 copy-start.3
  81.6 0.8 copy.26
  82.4 0.1 copy-done.3
  82.4 0.6 copy.27
Async XLA Ops:
  0.6 0.7 copy-start.4
  78.5 1.7 %copy-start.2 = (bf16[240,512]{1,0:T(8,128)(2,1)S(1)}, bf16[240,512]{1,0:T(8,128)(2,1)}, u32[]{:S(2)}) copy-start(bf16[240,512]{1,0:T(8,128)(2,1)} %get-tuple-element.21) | copy-start | bytes 737284
  78.5 2.4 %copy-start.1 = (bf16[240,512]{1,0:T(8,128)(2,1)S(1)}, bf16[240,512]{1,0:T(8,128)(2,1)}, u32[]{:S(2)}) copy-start(bf16[240,512]{1,0:T(8,128)(2,1)} %get-tuple-element.22) | copy-start | bytes 737284
  80.2 1.4 %copy-start = (f32[240,512]{1,0:T(8,128)S(1)}, f32[240,512]{1,0:T(8,128)}, u32[]{:S(2)}) copy-start(f32[240,512]{1,0:T(8,128)} %get-tuple-element.23) | copy-start | bytes 1474564
  81.6 0.9 %copy-start.3 = (f32[60,240]{1,0:T(8,128)S(1)}, f32[60,240]{1,0:T(8,128)}, u32[]{:S(2)}) copy-start(f32[60,240]{1,0:T(8,128)} %get-tuple-element.14) | copy-start | bytes 172804

commit v4 on v3

--- a/solution.py
+++ b/solution.py
@@ -19,7 +19,10 @@
 HALF = 256
 BATCH = 4
 LIMIT = 63 * 2**20
-CHUNKS = ((0, 64), (64, 64), (128, 64), (192, 48))
+CHUNKS = ((0, 48), (48, 32), (80, 48), (128, 32), (160, 48), (208, 32))
+FLIGHT = 3
+A1POS = 0
+OWNPOS = 2
 MESH = pl.DeviceIdType.MESH
 
 
@@ -134,11 +137,11 @@
     gate_hbm, key_hbm, value_hbm, filt_hbm, rate_hbm, weight_hbm, cotangent_hbm,
     first_hbm, twist_hbm, forward_hbm, backward_hbm, last_hbm,
     gate_grad, key_grad, value_grad, filter_grad, weight_grad,
-    gate, key, value, filt, rate, weight, first_in, twist, forward_in, backward_in, last_in,
+    gate, key, value, filt, rate_in, rate, weight, first_in, twist, forward_in, backward_in, last_in,
     first, forward, backward, last,
     send1, recv1, send2, recv2, send3, recv3, send4, recv4,
     gathered, upstream, envelope, rows1, rows2, specs, out1, out2, gated,
-    partial, core_in, chip_sum, x_in, x_sum, z_in, in_sem,
+    partial, core_in, chip_sum, x_in, x_sum, x_out, z_in, in_sem,
     ss1, rs1, ss2, rs2, ss3, rs3, ss4, rs4, ag_send, ag_recv, core_send, core_recv, x_send, x_recv, z_send, z_recv,
 ):
     me = lax.axis_index("seq")
@@ -164,7 +167,7 @@
                 (key_hbm, key),
                 (value_hbm, value),
                 (filt_hbm, filt),
-                (rate_hbm, rate),
+                (rate_hbm, rate_in),
                 (cotangent_hbm, gathered.at[own_rows]),
                 (gate_hbm, gate),
                 (first_hbm, first_in),
@@ -192,12 +195,14 @@
     position = (me * length + lax.broadcasted_iota(jnp.int32, (16, length), 1)).astype(F32)
     for load in loads[:4]:
         load.wait()
+    row = beside(rate_in[...], jnp.zeros((1, 2 * SIDE - blocks), F32))
+    rate[...] = jnp.broadcast_to(row, (SIDE, 2 * SIDE)).T
 
     @pl.loop(0, pairs)
     def _(p):
         r = pl.ds(pl.multiple_of(16 * p, 16), 16)
         sig = key[r, :].astype(F32) * value[r, :].astype(F32)
-        speed = rate[r, :]
+        speed = rate[r, :1]
         window = jnp.sqrt(1.0 - jnp.exp(-2.0 * speed)) * jnp.exp(-speed * position)
         envelope[r, :] = window
         ker = filt[r, :] * window
@@ -247,8 +252,8 @@
         go(gather_copy(3, far, c, above))
         go(gather_copy(4, far, c, below))
 
-    go(gather_copy(0, group, 0, far))
-    go(gather_copy(0, group, 1, far))
+    for c in span[:FLIGHT]:
+        go(gather_copy(0, group, c, far))
     for c in span:
         go(gather_copy(1, group, c, above))
         go(gather_copy(2, group, (c + middle) % len(CHUNKS), below))
@@ -260,19 +265,59 @@
         forward[rows, :] = forward_in[part].astype(BF16)
         backward[rows, :] = backward_in[part].astype(BF16)
         last[:, rows] = last_in[part].astype(BF16)
-    pass_far(0)
-    go(gather_copy(0, group, 2, far))
-    pass_far(1)
-    go(gather_copy(0, group, 3, far))
-    to_owners(send1, recv1, ss1, rs1)
+    if A1POS == 0:
+        to_owners(send1, recv1, ss1, rs1)
     for c in span:
-        land(relay(5, below, above, c))
-        go(relay(5, below, above, c))
-    pass_far(2)
-    pass_far(3)
+        pass_far(c)
+        if c + FLIGHT < len(CHUNKS):
+            go(gather_copy(0, group, c + FLIGHT, far))
+        if c + 1 == A1POS:
+            to_owners(send1, recv1, ss1, rs1)
+        if c + 1 == OWNPOS:
+            for d in span:
+                land(relay(5, below, above, d))
+                go(relay(5, below, above, d))
     for c in span:
         land(relay(6, below_far, above_far, c))
         go(relay(6, below_far, above_far, c))
+
+    @pl.when(owner)
+    def _():
+        @pl.loop(0, PIECES)
+        def _(s):
+            @pl.when(s != me)
+            def _():
+                land(arrival(s, send1, recv1, ss1, rs1))
+
+        @pl.loop(0, PIECES, unroll=4)
+        def _(s):
+            piece = recv1[s].astype(F32)
+            for i in range(4):
+                rows1[pl.ds(pl.multiple_of((s * 4 + i) * 16, 16), 16), :] = piece[:, i * SIDE : (i + 1) * SIDE]
+
+        @pl.loop(0, OWNED // BATCH)
+        def _(b):
+            cs = [b * BATCH + i for i in range(BATCH)]
+            sig = [rows1[pl.ds(c, SIDE, stride=16), :].astype(BF16) for c in cs]
+            ker = [rows1[pl.ds(c + 8, SIDE, stride=16), :].astype(BF16) for c in cs]
+            spec = forward_pair(jnp.concatenate(sig + ker, 1), first, twist, forward, 2 * BATCH)
+            specs[b] = spec
+            y = backward_pair(
+                product(spec[: SIDE * BATCH], spec[SIDE * BATCH :]), twist, backward, last, BATCH
+            )
+            for i, c in enumerate(cs):
+                out1[pl.ds(c, SIDE, stride=8), :] = y[:, i * SIDE : (i + 1) * SIDE]
+
+        @pl.loop(0, PIECES, unroll=4)
+        def _(s):
+            t = [out1[pl.ds(pl.multiple_of((s * 4 + i) * 8, 8), 8), :] for i in range(4)]
+            send3[s] = beside(stacked(t[0], t[2]), stacked(t[1], t[3])).astype(BF16)
+
+        @pl.loop(1, PIECES)
+        def _(k):
+            go(exchange(me, (me + k) % PIECES, send3, recv3, ss3, rs3))
+
+        recv3[me] = send3[me]
 
     for c in span:
         if c < middle:
@@ -298,43 +343,59 @@
 
     to_owners(send2, recv2, ss2, rs2)
 
-    @pl.when(owner)
-    def _():
-        @pl.loop(0, PIECES)
+    def from_owners(source, landing, send_sem, recv_sem):
+        @pl.loop(0, owners)
         def _(s):
             @pl.when(s != me)
             def _():
-                land(arrival(s, send1, recv1, ss1, rs1))
-
-        @pl.loop(0, PIECES, unroll=4)
-        def _(s):
-            piece = recv1[s].astype(F32)
-            for i in range(4):
-                rows1[pl.ds(pl.multiple_of((s * 4 + i) * 16, 16), 16), :] = piece[:, i * SIDE : (i + 1) * SIDE]
-
-        @pl.loop(0, OWNED // BATCH)
-        def _(b):
-            cs = [b * BATCH + i for i in range(BATCH)]
-            sig = [rows1[pl.ds(c, SIDE, stride=16), :].astype(BF16) for c in cs]
-            ker = [rows1[pl.ds(c + 8, SIDE, stride=16), :].astype(BF16) for c in cs]
-            spec = forward_pair(jnp.concatenate(sig + ker, 1), first, twist, forward, 2 * BATCH)
-            specs[b] = spec
-            y = backward_pair(
-                product(spec[: SIDE * BATCH], spec[SIDE * BATCH :]), twist, backward, last, BATCH
-            )
-            for i, c in enumerate(cs):
-                out1[pl.ds(c, SIDE, stride=8), :] = y[:, i * SIDE : (i + 1) * SIDE]
-
-        @pl.loop(0, PIECES, unroll=4)
-        def _(s):
-            t = [out1[pl.ds(pl.multiple_of((s * 4 + i) * 8, 8), 8), :] for i in range(4)]
-            send3[s] = beside(stacked(t[0], t[2]), stacked(t[1], t[3])).astype(BF16)
-
-        @pl.loop(1, PIECES)
-        def _(k):
-            go(exchange(me, (me + k) % PIECES, send3, recv3, ss3, rs3))
-
-        recv3[me] = send3[me]
+                land(arrival(s, source, landing, send_sem, recv_sem))
+
+    from_owners(send3, recv3, ss3, rs3)
+
+    @pl.loop(0, pairs)
+    def _(p):
+        r = pl.ds(pl.multiple_of(16 * p, 16), 16)
+        a = recv3[2 * p].astype(F32)
+        b = recv3[2 * p + 1].astype(F32)
+        conv = stacked(beside(a[:8], a[8:]), beside(b[:8], b[8:]))
+        gate_grad[r, :] = (upstream[r, :] * conv).astype(BF16)
+        high, low = split(gate[r, :].astype(F32) * conv)
+        gated[r, :] = beside(high, low)
+
+    for j in range(GROUPS):
+        rows = gathered[pl.ds(blocks * j, HALF), :]
+        term = lax.dot_general(
+            beside(rows, rows), gated[...], (((1,), (1,)), ((), ())), preferred_element_type=F32
+        )
+        for g in range(4):
+            partial[g % 2, 2 * j + g // 2] = term[60 * g : 60 * g + 64]
+
+    core_copy = pltpu.make_async_remote_copy(
+        src_ref=partial.at[1 - core],
+        dst_ref=core_in,
+        send_sem=core_send,
+        recv_sem=core_recv,
+        device_id={"seq": sibling},
+        device_id_type=MESH,
+    )
+    go(core_copy)
+
+    def x_copy(k):
+        there = (x + k) % 4
+        return pltpu.make_async_remote_copy(
+            src_ref=chip_sum.at[pl.ds(4 * there, 4)],
+            dst_ref=x_in.at[k - 1],
+            send_sem=x_send.at[k - 1],
+            recv_sem=x_recv.at[k - 1],
+            device_id={"seq": (me + 8 * k) % PIECES},
+            device_id_type=MESH,
+        )
+
+    land(core_copy)
+    partial[core] = partial[core] + core_in[...]
+    chip_sum[...] = partial[core].astype(BF16)
+    for k in (1, 2, 3):
+        go(x_copy(k))
 
     @pl.when(owner)
     def _():
@@ -353,8 +414,9 @@
                     h * 8 : h * 8 + 8, l * SIDE : (l + 1) * SIDE
                 ]
 
-        @pl.loop(0, OWNED // BATCH)
-        def _(b):
+    def correlate(b):
+        @pl.when(owner)
+        def _():
             cs = [b * BATCH + i for i in range(BATCH)]
             g = [rows2[pl.ds(c, SIDE, stride=8), :].astype(BF16) for c in cs]
             gspec = forward_pair(jnp.concatenate(g, 1), first, twist, forward, BATCH)
@@ -377,59 +439,9 @@
 
             recv4[b, me] = send4[b, me]
 
-    def from_owners(source, landing, send_sem, recv_sem):
-        @pl.loop(0, owners)
-        def _(s):
-            @pl.when(s != me)
-            def _():
-                land(arrival(s, source, landing, send_sem, recv_sem))
-
-    from_owners(send3, recv3, ss3, rs3)
-
-    @pl.loop(0, pairs)
-    def _(p):
-        r = pl.ds(pl.multiple_of(16 * p, 16), 16)
-        a = recv3[2 * p].astype(F32)
-        b = recv3[2 * p + 1].astype(F32)
-        conv = stacked(beside(a[:8], a[8:]), beside(b[:8], b[8:]))
-        gate_grad[r, :] = (upstream[r, :] * conv).astype(BF16)
-        high, low = split(gate[r, :].astype(F32) * conv)
-        gated[r, :] = beside(high, low)
-
-    for j in range(GROUPS):
-        rows = gathered[pl.ds(blocks * j, HALF), :]
-        term = lax.dot_general(
-            beside(rows, rows), gated[...], (((1,), (1,)), ((), ())), preferred_element_type=F32
-        )
-        for g in range(4):
-            partial[g % 2, 2 * j + g // 2] = term[60 * g : 60 * g + 64]
-
-    core_copy = pltpu.make_async_remote_copy(
-        src_ref=partial.at[1 - core],
-        dst_ref=core_in,
-        send_sem=core_send,
-        recv_sem=core_recv,
-        device_id={"seq": sibling},
-        device_id_type=MESH,
-    )
-    go(core_copy)
-
-    def x_copy(k):
-        there = (x + k) % 4
-        return pltpu.make_async_remote_copy(
-            src_ref=chip_sum.at[pl.ds(4 * there, 4)],
-            dst_ref=x_in.at[k - 1],
-            send_sem=x_send.at[k - 1],
-            recv_sem=x_recv.at[k - 1],
-            device_id={"seq": (me + 8 * k) % PIECES},
-            device_id_type=MESH,
-        )
-
-    land(core_copy)
-    partial[core] = partial[core] + core_in[...]
-    chip_sum[...] = partial[core].astype(BF16)
-    for k in (1, 2, 3):
-        go(x_copy(k))
+    correlate(0)
+
+    correlate(1)
 
     for k in (1, 2, 3):
         land(x_copy(k))
@@ -438,7 +450,7 @@
     def z_copy(k):
         there = (z + k) % 4
         return pltpu.make_async_remote_copy(
-            src_ref=x_sum.at[there],
+            src_ref=x_out.at[there],
             dst_ref=z_in.at[k - 1],
             send_sem=z_send.at[k - 1],
             recv_sem=z_recv.at[k - 1],
@@ -446,6 +458,7 @@
             device_id_type=MESH,
         )
 
+    x_out[...] = x_sum[...].astype(BF16)
     for k in (1, 2, 3):
         go(z_copy(k))
 
@@ -468,7 +481,7 @@
 
     for k in (1, 2, 3):
         land(z_copy(k))
-    total = x_sum[z] + z_in[0] + z_in[1] + z_in[2]
+    total = x_sum[z] + z_in[0].astype(F32) + z_in[1].astype(F32) + z_in[2].astype(F32)
     weight_grad[...] = total[: weight_grad.shape[0], :blocks]
 
     for k in (1, 2, 3):
@@ -500,6 +513,20 @@
                 leave(exchange(me, target, send4.at[b], recv4.at[b], ss4.at[b], rs4.at[b]))
 
 
+def settle_kernel(*refs):
+    count = len(refs) // 3
+    arrivals, departures = refs[-2], refs[-1]
+    inward = [pltpu.make_async_copy(refs[i], refs[2 * count + i], arrivals.at[i]) for i in range(count)]
+    outward = [pltpu.make_async_copy(refs[2 * count + i], refs[count + i], departures.at[i]) for i in range(count)]
+    for copy in inward:
+        copy.start()
+    for copy, onward in zip(inward, outward):
+        copy.wait()
+        onward.start()
+    for onward in outward:
+        onward.wait()
+
+
 def per_device(gate_act, key_act, value_act, filter_raw, decay_rate, out_weight, out_grad):
     channels, length = gate_act.shape
     tables = [jnp.asarray(t) for t in make_tables()]
@@ -507,7 +534,7 @@
     vmem = pltpu.VMEM
     dma = pltpu.SemaphoreType.DMA
     rows = SIDE * OWNED
-    *grads, weight_grad = pl.pallas_call(
+    results = pl.pallas_call(
         whole_kernel,
         out_shape=(
             jax.ShapeDtypeStruct(shape, BF16),
@@ -522,7 +549,8 @@
             vmem(shape, BF16),
             vmem(shape, BF16),
             vmem(shape, F32),
-            vmem((channels, 1), F32),
+            vmem((1, channels), F32),
+            vmem((2 * SIDE, SIDE), F32),
             vmem(out_weight.shape, BF16),
         ]
         + [vmem(t.shape, t.dtype) for t in tables]
@@ -553,7 +581,8 @@
             vmem((16, 64, HALF), BF16),
             vmem((3, 4, 64, HALF), BF16),
             vmem((4, 64, HALF), F32),
-            vmem((3, 64, HALF), F32),
+            vmem((4, 64, HALF), BF16),
+            vmem((3, 64, HALF), BF16),
             dma((12,)),
         ]
         + [dma((PIECES,))] * 6
@@ -563,7 +592,15 @@
         compiler_params=pltpu.CompilerParams(
             collective_id=0, has_side_effects=True, vmem_limit_bytes=LIMIT
         ),
-    )(gate_act, key_act, value_act, filter_raw, decay_rate[:, None], out_weight, out_grad, *tables)
+    )(gate_act, key_act, value_act, filter_raw, decay_rate[None, :], out_weight, out_grad, *tables)
+    *grads, weight_grad = pl.pallas_call(
+        settle_kernel,
+        out_shape=tuple(jax.ShapeDtypeStruct(r.shape, r.dtype) for r in results),
+        in_specs=[pl.BlockSpec(memory_space=pltpu.HBM)] * 5,
+        out_specs=[pl.BlockSpec(memory_space=pltpu.HBM)] * 5,
+        scratch_shapes=[vmem(r.shape, r.dtype) for r in results] + [dma((5,))] * 2,
+        compiler_params=pltpu.CompilerParams(vmem_limit_bytes=LIMIT),
+    )(*results)
     return (*grads, weight_grad.T)
 
 

time: 83.2 us -> 78 us (0.938)
  local copies, waits for them, and re-layouts: 6.06 us -> 0 us
  Pallas kernels: 76.3 us -> 77.3 us
    unnamed x15 -> x0, local copies, waits for them, and re-layouts: 5.27 us -> none
    pallas_call x0 -> x1, Pallas kernels: none -> 2.28 us  [per_device(): pl.pallas_call(settle_kernel, out_shape=tuple((jax.ShapeDtypeStruct(r.sha...]
    pallas_call x1, Pallas kernels: 76.3 us -> 75 us  [per_device(): pl.pallas_call(whole_kernel, out_shape=(jax.ShapeDtypeStruct(shape, BF16)...]
where the time goes in v4:
time: 78 us; the launch traced here: 77.9 us
  Pallas kernels  77.3 us (99%)
    pallas_call x1, Pallas kernels, per_device(): pl.pallas_call(whole_kernel, out_shape=(jax.ShapeDtypeStruct(shape, BF16)...  75 us
    pallas_call x1, Pallas kernels, per_device(): pl.pallas_call(settle_kernel, out_shape=tuple((jax.ShapeDtypeStruct(r.sha...  2.28 us

profile of v4, /device:TPU:16, one launch (start us, length us, event | category | flops | bytes accessed | tf_op | source)
XLA Modules:
  0.0 77.9 jit_solution(5602200579518219081)
XLA Ops:
  0.6 75.0 %shard_map.155 = (bf16[240,512]{1,0:T(8,128)(2,1)}, bf16[240,512]{1,0:T(8,128)(2,1)}, bf16[240,512]{1,0:T(8,128)(2,1)}, f32[240,512]{1,0:T(8,128)}, f32[60,240]{1,0:T(8,128)}) custom-call(bf16[240,512]{1,0:T(8,128)(2,1)} %gate_hbm.1, bf16[240,512]{1,0:T(8,128)(2,1)} %key_hbm.1, bf16[240,512]{1,0:T(8,128)(2,1)} %value_hbm.1, f32[240,512]{1,0:T(8,128)} %filt_hbm.1, ...), custom_call_target="tpu_custom_call" | custom-call | tf_op jit(solution)/shard_map/pallas_call | solution.py:537
  75.6 2.3 %shard_map.156 = (bf16[240,512]{1,0:T(8,128)(2,1)}, bf16[240,512]{1,0:T(8,128)(2,1)}, bf16[240,512]{1,0:T(8,128)(2,1)}, f32[240,512]{1,0:T(8,128)}, f32[60,240]{1,0:T(8,128)}) custom-call(bf16[240,512]{1,0:T(8,128)(2,1)} %get-tuple-element.15.refs_0_, bf16[240,512]{1,0:T(8,128)(2,1)} %get-tuple-element.16.refs_1_, ...), custom_call_target="tpu_custom_call" | custom-call | tf_op jit(solution)/shard_map/pallas_call | solution.py:596

commit v5 on v4

--- a/solution.py
+++ b/solution.py
@@ -18,6 +18,7 @@
 GROUPS = 8
 HALF = 256
 BATCH = 4
+THIRDS = 3
 LIMIT = 63 * 2**20
 CHUNKS = ((0, 48), (48, 32), (80, 48), (128, 32), (160, 48), (208, 32))
 FLIGHT = 3
@@ -114,15 +115,30 @@
     return pltpu.make_async_remote_copy(
         src_ref=source.at[target],
         dst_ref=landing.at[me],
-        send_sem=send_sem.at[target],
-        recv_sem=recv_sem.at[me],
+        send_sem=send_sem,
+        recv_sem=recv_sem,
         device_id={"seq": target},
         device_id_type=MESH,
     )
 
 
-def arrival(origin, source, landing, send_sem, recv_sem):
-    return exchange(origin, origin, source, landing, send_sem, recv_sem)
+def all_of(count, peer, source, landing, send_sem, recv_sem):
+    return pltpu.make_async_remote_copy(
+        src_ref=source.at[pl.ds(0, count)],
+        dst_ref=landing.at[pl.ds(0, count)],
+        send_sem=send_sem,
+        recv_sem=recv_sem,
+        device_id={"seq": peer},
+        device_id_type=MESH,
+    )
+
+
+def third(source, target, sem, index, part):
+    total = source.shape[0]
+    count = total // THIRDS // 8 * 8
+    begin = part * count
+    rows = pl.ds(begin, count if part < THIRDS - 1 else total - begin)
+    return pltpu.make_async_copy(source.at[rows], target.at[rows], sem.at[index, part])
 
 
 def stacked(upper, lower):
@@ -136,7 +152,8 @@
 def whole_kernel(
     gate_hbm, key_hbm, value_hbm, filt_hbm, rate_hbm, weight_hbm, cotangent_hbm,
     first_hbm, twist_hbm, forward_hbm, backward_hbm, last_hbm,
-    gate_grad, key_grad, value_grad, filter_grad, weight_grad,
+    gate_grad_hbm, key_grad_hbm, value_grad_hbm, filter_grad_hbm, weight_grad_hbm,
+    gate_grad, key_grad, value_grad, filter_grad, weight_grad, out_sem,
     gate, key, value, filt, rate_in, rate, weight, first_in, twist, forward_in, backward_in, last_in,
     first, forward, backward, last,
     send1, recv1, send2, recv2, send3, recv3, send4, recv4,
@@ -212,13 +229,13 @@
     loads[4].wait()
     pl.semaphore_wait(barrier, PIECES - 1 + 3)
 
-    def gather_copy(index, slot, chunk, target):
+    def gather_copy(slot, chunk, target):
         begin, count = CHUNKS[chunk]
         rows = gathered.at[pl.ds(pl.multiple_of(blocks * slot + begin, 16), count)]
         return pltpu.make_async_remote_copy(
             src_ref=rows,
             dst_ref=rows,
-            send_sem=ag_send.at[index, chunk],
+            send_sem=ag_send,
             recv_sem=ag_recv.at[slot, chunk],
             device_id={"chan": target},
             device_id_type=MESH,
@@ -229,10 +246,10 @@
     above_far = above + 1 - 2 * (above % 2)
     below_far = below + 1 - 2 * (below % 2)
 
-    def relay(index, from_below, from_above, chunk):
+    def relay(from_below, from_above, chunk):
         if chunk < middle:
-            return gather_copy(index, from_below, chunk, above)
-        return gather_copy(index, from_above, chunk, below)
+            return gather_copy(from_below, chunk, above)
+        return gather_copy(from_above, chunk, below)
 
     def to_owners(source, landing, send_sem, recv_sem):
         @pl.loop(1, PIECES)
@@ -248,15 +265,15 @@
             landing[me] = source[me]
 
     def pass_far(c):
-        land(gather_copy(0, far, c, far))
-        go(gather_copy(3, far, c, above))
-        go(gather_copy(4, far, c, below))
+        land(gather_copy(far, c, far))
+        go(gather_copy(far, c, above))
+        go(gather_copy(far, c, below))
 
     for c in span[:FLIGHT]:
-        go(gather_copy(0, group, c, far))
+        go(gather_copy(group, c, far))
     for c in span:
-        go(gather_copy(1, group, c, above))
-        go(gather_copy(2, group, (c + middle) % len(CHUNKS), below))
+        go(gather_copy(group, c, above))
+        go(gather_copy(group, (c + middle) % len(CHUNKS), below))
     for load in loads[5:]:
         load.wait()
     first[...] = first_in[...].astype(BF16)
@@ -270,24 +287,20 @@
     for c in span:
         pass_far(c)
         if c + FLIGHT < len(CHUNKS):
-            go(gather_copy(0, group, c + FLIGHT, far))
+            go(gather_copy(group, c + FLIGHT, far))
         if c + 1 == A1POS:
             to_owners(send1, recv1, ss1, rs1)
         if c + 1 == OWNPOS:
             for d in span:
-                land(relay(5, below, above, d))
-                go(relay(5, below, above, d))
+                land(relay(below, above, d))
+                go(relay(below, above, d))
     for c in span:
-        land(relay(6, below_far, above_far, c))
-        go(relay(6, below_far, above_far, c))
+        land(relay(below_far, above_far, c))
+        go(relay(below_far, above_far, c))
 
     @pl.when(owner)
     def _():
-        @pl.loop(0, PIECES)
-        def _(s):
-            @pl.when(s != me)
-            def _():
-                land(arrival(s, send1, recv1, ss1, rs1))
+        land(all_of(PIECES - 1, sibling, send1, recv1, ss1, rs1))
 
         @pl.loop(0, PIECES, unroll=4)
         def _(s):
@@ -321,14 +334,14 @@
 
     for c in span:
         if c < middle:
-            land(gather_copy(0, above, c, above))
-            land(gather_copy(0, above_far, c, above))
+            land(gather_copy(above, c, above))
+            land(gather_copy(above_far, c, above))
         else:
-            land(gather_copy(0, below, c, below))
-            land(gather_copy(0, below_far, c, below))
+            land(gather_copy(below, c, below))
+            land(gather_copy(below_far, c, below))
         opposite = (group + 4) % GROUPS
-        land(gather_copy(0, opposite, c, above))
-        land(gather_copy(0, opposite + 1 - 2 * (opposite % 2), c, above))
+        land(gather_copy(opposite, c, above))
+        land(gather_copy(opposite + 1 - 2 * (opposite % 2), c, above))
     depth = blocks * GROUPS
     for n in range(length // HALF):
         cols = pl.ds(n * HALF, HALF)
@@ -344,11 +357,13 @@
     to_owners(send2, recv2, ss2, rs2)
 
     def from_owners(source, landing, send_sem, recv_sem):
-        @pl.loop(0, owners)
-        def _(s):
-            @pl.when(s != me)
-            def _():
-                land(arrival(s, source, landing, send_sem, recv_sem))
+        @pl.when(owner)
+        def _():
+            land(all_of(owners - 1, sibling, source, landing, send_sem, recv_sem))
+
+        @pl.when(me >= owners)
+        def _():
+            land(all_of(owners, sibling, source, landing, send_sem, recv_sem))
 
     from_owners(send3, recv3, ss3, rs3)
 
@@ -361,6 +376,9 @@
         gate_grad[r, :] = (upstream[r, :] * conv).astype(BF16)
         high, low = split(gate[r, :].astype(F32) * conv)
         gated[r, :] = beside(high, low)
+
+    for t in range(THIRDS):
+        third(gate_grad, gate_grad_hbm, out_sem, 0, t).start()
 
     for j in range(GROUPS):
         rows = gathered[pl.ds(blocks * j, HALF), :]
@@ -399,11 +417,7 @@
 
     @pl.when(owner)
     def _():
-        @pl.loop(0, PIECES)
-        def _(s):
-            @pl.when(s != me)
-            def _():
-                land(arrival(s, send2, recv2, ss2, rs2))
+        land(all_of(PIECES - 1, sibling, send2, recv2, ss2, rs2))
 
         @pl.loop(0, PIECES, unroll=4)
         def _(s):
@@ -465,59 +479,75 @@
     for b in range(2):
         from_owners(send4.at[b], recv4.at[b], ss4.at[b], rs4.at[b])
 
-    @pl.loop(0, pairs)
-    def _(p):
-        r = pl.ds(pl.multiple_of(16 * p, 16), 16)
-        parts = []
-        for o in range(2):
-            for b in range(2):
-                a = recv4[b, 2 * p + o].astype(F32)
-                parts.append(beside(a[:8], a[8:]))
-        sgrad = jnp.concatenate([a[:4] for a in parts], 0)
-        kgrad = jnp.concatenate([a[4:] for a in parts], 0)
-        key_grad[r, :] = (sgrad * value[r, :].astype(F32)).astype(BF16)
-        value_grad[r, :] = (sgrad * key[r, :].astype(F32)).astype(BF16)
-        filter_grad[r, :] = kgrad * envelope[r, :]
+    outs = ((key_grad, key_grad_hbm), (value_grad, value_grad_hbm), (filter_grad, filter_grad_hbm))
+    for t in range(THIRDS):
+        @pl.loop(t * pairs // THIRDS, (t + 1) * pairs // THIRDS)
+        def _(p):
+            r = pl.ds(pl.multiple_of(16 * p, 16), 16)
+            parts = []
+            for o in range(2):
+                for b in range(2):
+                    a = recv4[b, 2 * p + o].astype(F32)
+                    parts.append(beside(a[:8], a[8:]))
+            sgrad = jnp.concatenate([a[:4] for a in parts], 0)
+            kgrad = jnp.concatenate([a[4:] for a in parts], 0)
+            key_grad[r, :] = (sgrad * value[r, :].astype(F32)).astype(BF16)
+            value_grad[r, :] = (sgrad * key[r, :].astype(F32)).astype(BF16)
+            filter_grad[r, :] = kgrad * envelope[r, :]
+
+        for n, (source, target) in enumerate(outs):
+            third(source, target, out_sem, 1 + n, t).start()
 
     for k in (1, 2, 3):
         land(z_copy(k))
     total = x_sum[z] + z_in[0].astype(F32) + z_in[1].astype(F32) + z_in[2].astype(F32)
     weight_grad[...] = total[: weight_grad.shape[0], :blocks]
+    weight_out = pltpu.make_async_copy(weight_grad, weight_grad_hbm, out_sem.at[4, 0])
+    weight_out.start()
 
     for k in (1, 2, 3):
         leave(x_copy(k))
         leave(z_copy(k))
     leave(core_copy)
-    for c in span:
-        leave(gather_copy(0, group, c, far))
-        leave(gather_copy(1, group, c, above))
-        leave(gather_copy(2, group, c, below))
-        leave(gather_copy(3, far, c, above))
-        leave(gather_copy(4, far, c, below))
-        leave(relay(5, below, above, c))
-        leave(relay(6, below_far, above_far, c))
-
-    @pl.loop(1, PIECES)
-    def _(k):
-        target = (me + k) % PIECES
-
-        @pl.when(target < owners)
-        def _():
-            leave(exchange(me, target, send1, recv1, ss1, rs1))
-            leave(exchange(me, target, send2, recv2, ss2, rs2))
-
-        @pl.when(owner)
-        def _():
-            leave(exchange(me, target, send3, recv3, ss3, rs3))
-            for b in range(2):
-                leave(exchange(me, target, send4.at[b], recv4.at[b], ss4.at[b], rs4.at[b]))
+    sent = gathered.at[pl.ds(0, 7 * blocks)]
+    leave(
+        pltpu.make_async_remote_copy(
+            src_ref=sent,
+            dst_ref=sent,
+            send_sem=ag_send,
+            recv_sem=ag_recv.at[0, 0],
+            device_id={"chan": far},
+            device_id_type=MESH,
+        )
+    )
+
+    @pl.when(owner)
+    def _():
+        leave(all_of(owners - 1, sibling, send1, recv1, ss1, rs1))
+        leave(all_of(owners - 1, sibling, send2, recv2, ss2, rs2))
+        leave(all_of(PIECES - 1, sibling, send3, recv3, ss3, rs3))
+        for b in range(2):
+            leave(all_of(PIECES - 1, sibling, send4.at[b], recv4.at[b], ss4.at[b], rs4.at[b]))
+
+    @pl.when(me >= owners)
+    def _():
+        leave(all_of(owners, sibling, send1, recv1, ss1, rs1))
+        leave(all_of(owners, sibling, send2, recv2, ss2, rs2))
+
+    for t in range(THIRDS):
+        third(gate_grad, gate_grad_hbm, out_sem, 0, t).wait()
+        for n, (source, target) in enumerate(outs):
+            third(source, target, out_sem, 1 + n, t).wait()
+    weight_out.wait()
 
 
 def settle_kernel(*refs):
     count = len(refs) // 3
-    arrivals, departures = refs[-2], refs[-1]
-    inward = [pltpu.make_async_copy(refs[i], refs[2 * count + i], arrivals.at[i]) for i in range(count)]
-    outward = [pltpu.make_async_copy(refs[2 * count + i], refs[count + i], departures.at[i]) for i in range(count)]
+    inward, outward = [], []
+    for i in range(count):
+        for t in range(THIRDS):
+            inward.append(third(refs[i], refs[2 * count + i], refs[-2], i, t))
+            outward.append(third(refs[2 * count + i], refs[count + i], refs[-1], i, t))
     for copy in inward:
         copy.start()
     for copy, onward in zip(inward, outward):
@@ -544,7 +574,14 @@
             jax.ShapeDtypeStruct((channels * GROUPS // PIECES, channels), F32),
         ),
         in_specs=[pl.BlockSpec(memory_space=pltpu.HBM)] * 12,
+        out_specs=(pl.BlockSpec(memory_space=pltpu.HBM),) * 5,
         scratch_shapes=[
+            vmem(shape, BF16),
+            vmem(shape, BF16),
+            vmem(shape, BF16),
+            vmem(shape, F32),
+            vmem((channels * GROUPS // PIECES, channels), F32),
+            dma((5, THIRDS)),
             vmem(shape, BF16),
             vmem(shape, BF16),
             vmem(shape, BF16),
@@ -585,9 +622,9 @@
             vmem((3, 64, HALF), BF16),
             dma((12,)),
         ]
-        + [dma((PIECES,))] * 6
-        + [dma((2, PIECES))] * 2
-        + [dma((7, len(CHUNKS))), dma((GROUPS, len(CHUNKS))), dma, dma]
+        + [dma] * 6
+        + [dma((2,))] * 2
+        + [dma, dma((GROUPS, len(CHUNKS))), dma, dma]
         + [dma((3,))] * 4,
         compiler_params=pltpu.CompilerParams(
             collective_id=0, has_side_effects=True, vmem_limit_bytes=LIMIT
@@ -598,7 +635,7 @@
         out_shape=tuple(jax.ShapeDtypeStruct(r.shape, r.dtype) for r in results),
         in_specs=[pl.BlockSpec(memory_space=pltpu.HBM)] * 5,
         out_specs=[pl.BlockSpec(memory_space=pltpu.HBM)] * 5,
-        scratch_shapes=[vmem(r.shape, r.dtype) for r in results] + [dma((5,))] * 2,
+        scratch_shapes=[vmem(r.shape, r.dtype) for r in results] + [dma((5, THIRDS))] * 2,
         compiler_params=pltpu.CompilerParams(vmem_limit_bytes=LIMIT),
     )(*results)
     return (*grads, weight_grad.T)

time: 78 us -> 73.3 us (0.940)
  Pallas kernels: 77.3 us -> 72.5 us
    pallas_call x1, Pallas kernels: 75 us -> 70.2 us  [per_device(): pl.pallas_call(whole_kernel, out_shape=(jax.ShapeDtypeStruct(shape, BF16)...]
where the time goes in v5:
time: 73.3 us; the launch traced here: 73.1 us
  Pallas kernels  72.5 us (99%)
    pallas_call x1, Pallas kernels, per_device(): pl.pallas_call(whole_kernel, out_shape=(jax.ShapeDtypeStruct(shape, BF16)...  70.2 us
    pallas_call x1, Pallas kernels, per_device(): pl.pallas_call(settle_kernel, out_shape=tuple((jax.ShapeDtypeStruct(r.sha...  2.3 us

profile of v5, /device:TPU:16, one launch (start us, length us, event | category | flops | bytes accessed | tf_op | source)
XLA Modules:
  0.0 73.1 jit_solution(6298440742536733460)
XLA Ops:
  0.6 70.2 %shard_map.155 = (bf16[240,512]{1,0:T(8,128)(2,1)}, bf16[240,512]{1,0:T(8,128)(2,1)}, bf16[240,512]{1,0:T(8,128)(2,1)}, f32[240,512]{1,0:T(8,128)}, f32[60,240]{1,0:T(8,128)}) custom-call(bf16[240,512]{1,0:T(8,128)(2,1)} %gate_hbm.1, bf16[240,512]{1,0:T(8,128)(2,1)} %key_hbm.1, bf16[240,512]{1,0:T(8,128)(2,1)} %value_hbm.1, f32[240,512]{1,0:T(8,128)} %filt_hbm.1, ...), custom_call_target="tpu_custom_call" | custom-call | tf_op jit(solution)/shard_map/pallas_call | solution.py:567
  70.8 2.3 %shard_map.156 = (bf16[240,512]{1,0:T(8,128)(2,1)}, bf16[240,512]{1,0:T(8,128)(2,1)}, bf16[240,512]{1,0:T(8,128)(2,1)}, f32[240,512]{1,0:T(8,128)}, f32[60,240]{1,0:T(8,128)}) custom-call(bf16[240,512]{1,0:T(8,128)(2,1)} %get-tuple-element.15.refs_0_, bf16[240,512]{1,0:T(8,128)(2,1)} %get-tuple-element.16.refs_1_, ...), custom_call_target="tpu_custom_call" | custom-call | tf_op jit(solution)/shard_map/pallas_call | solution.py:633

commit v6 on v5

--- a/solution.py
+++ b/solution.py
@@ -22,7 +22,7 @@
 LIMIT = 63 * 2**20
 CHUNKS = ((0, 48), (48, 32), (80, 48), (128, 32), (160, 48), (208, 32))
 FLIGHT = 3
-A1POS = 0
+A1POS = 2
 OWNPOS = 2
 MESH = pl.DeviceIdType.MESH
 
@@ -318,19 +318,18 @@
             y = backward_pair(
                 product(spec[: SIDE * BATCH], spec[SIDE * BATCH :]), twist, backward, last, BATCH
             )
-            for i, c in enumerate(cs):
-                out1[pl.ds(c, SIDE, stride=8), :] = y[:, i * SIDE : (i + 1) * SIDE]
-
-        @pl.loop(0, PIECES, unroll=4)
-        def _(s):
-            t = [out1[pl.ds(pl.multiple_of((s * 4 + i) * 8, 8), 8), :] for i in range(4)]
-            send3[s] = beside(stacked(t[0], t[2]), stacked(t[1], t[3])).astype(BF16)
-
-        @pl.loop(1, PIECES)
-        def _(k):
-            go(exchange(me, (me + k) % PIECES, send3, recv3, ss3, rs3))
-
-        recv3[me] = send3[me]
+            for i in range(BATCH):
+                out1[pl.ds(i, SIDE, stride=BATCH), :] = y[:, i * SIDE : (i + 1) * SIDE]
+
+            @pl.loop(0, PIECES, unroll=4)
+            def _(s):
+                send3[b, s] = out1[pl.ds(pl.multiple_of(s * 16, 16), 16), :].astype(BF16)
+
+            @pl.loop(1, PIECES)
+            def _(k):
+                go(exchange(me, (me + k) % PIECES, send3.at[b], recv3.at[b], ss3.at[b], rs3.at[b]))
+
+            recv3[b, me] = send3[b, me]
 
     for c in span:
         if c < middle:
@@ -351,10 +350,14 @@
     def _(p):
         r = pl.ds(pl.multiple_of(16 * p, 16), 16)
         g = upstream[r, :] * gate[r, :].astype(F32)
-        send2[2 * p] = stacked(g[:8, :HALF], g[:8, HALF:]).astype(BF16)
-        send2[2 * p + 1] = stacked(g[8:, :HALF], g[8:, HALF:]).astype(BF16)
-
-    to_owners(send2, recv2, ss2, rs2)
+        for o in range(2):
+            for b in range(2):
+                q = g[8 * o + 4 * b : 8 * o + 4 * b + 4]
+                quarters = [q[:, i * SIDE : (i + 1) * SIDE] for i in range(4)]
+                send2[b, 2 * p + o] = jnp.concatenate(quarters, 0).astype(BF16)
+
+    for b in range(2):
+        to_owners(send2.at[b], recv2.at[b], ss2.at[b], rs2.at[b])
 
     def from_owners(source, landing, send_sem, recv_sem):
         @pl.when(owner)
@@ -365,14 +368,18 @@
         def _():
             land(all_of(owners, sibling, source, landing, send_sem, recv_sem))
 
-    from_owners(send3, recv3, ss3, rs3)
+    for b in range(2):
+        from_owners(send3.at[b], recv3.at[b], ss3.at[b], rs3.at[b])
 
     @pl.loop(0, pairs)
     def _(p):
         r = pl.ds(pl.multiple_of(16 * p, 16), 16)
-        a = recv3[2 * p].astype(F32)
-        b = recv3[2 * p + 1].astype(F32)
-        conv = stacked(beside(a[:8], a[8:]), beside(b[:8], b[8:]))
+        parts = []
+        for o in range(2):
+            for b in range(2):
+                a = recv3[b, 2 * p + o].astype(F32)
+                parts.append(jnp.concatenate([a[4 * i : 4 * i + 4] for i in range(4)], 1))
+        conv = jnp.concatenate(parts, 0)
         gate_grad[r, :] = (upstream[r, :] * conv).astype(BF16)
         high, low = split(gate[r, :].astype(F32) * conv)
         gated[r, :] = beside(high, low)
@@ -415,24 +422,16 @@
     for k in (1, 2, 3):
         go(x_copy(k))
 
-    @pl.when(owner)
-    def _():
-        land(all_of(PIECES - 1, sibling, send2, recv2, ss2, rs2))
-
-        @pl.loop(0, PIECES, unroll=4)
-        def _(s):
-            piece = recv2[s].astype(F32)
-            for i in range(4):
-                h, l = i // 2, i % 2
-                rows2[pl.ds(pl.multiple_of((s * 4 + i) * 8, 8), 8), :] = piece[
-                    h * 8 : h * 8 + 8, l * SIDE : (l + 1) * SIDE
-                ]
-
     def correlate(b):
         @pl.when(owner)
         def _():
-            cs = [b * BATCH + i for i in range(BATCH)]
-            g = [rows2[pl.ds(c, SIDE, stride=8), :].astype(BF16) for c in cs]
+            land(all_of(PIECES - 1, sibling, send2.at[b], recv2.at[b], ss2.at[b], rs2.at[b]))
+
+            @pl.loop(0, PIECES, unroll=4)
+            def _(s):
+                rows2[pl.ds(pl.multiple_of(s * 16, 16), 16), :] = recv2[b, s].astype(F32)
+
+            g = [rows2[pl.ds(i, SIDE, stride=BATCH), :].astype(BF16) for i in range(BATCH)]
             gspec = forward_pair(jnp.concatenate(g, 1), first, twist, forward, BATCH)
             spec = specs[b]
             both = stacked(
@@ -524,15 +523,16 @@
     @pl.when(owner)
     def _():
         leave(all_of(owners - 1, sibling, send1, recv1, ss1, rs1))
-        leave(all_of(owners - 1, sibling, send2, recv2, ss2, rs2))
-        leave(all_of(PIECES - 1, sibling, send3, recv3, ss3, rs3))
         for b in range(2):
+            leave(all_of(owners - 1, sibling, send2.at[b], recv2.at[b], ss2.at[b], rs2.at[b]))
+            leave(all_of(PIECES - 1, sibling, send3.at[b], recv3.at[b], ss3.at[b], rs3.at[b]))
             leave(all_of(PIECES - 1, sibling, send4.at[b], recv4.at[b], ss4.at[b], rs4.at[b]))
 
     @pl.when(me >= owners)
     def _():
         leave(all_of(owners, sibling, send1, recv1, ss1, rs1))
-        leave(all_of(owners, sibling, send2, recv2, ss2, rs2))
+        for b in range(2):
+            leave(all_of(owners, sibling, send2.at[b], recv2.at[b], ss2.at[b], rs2.at[b]))
 
     for t in range(THIRDS):
         third(gate_grad, gate_grad_hbm, out_sem, 0, t).wait()
@@ -598,19 +598,19 @@
             vmem((SIDE, 6 * SIDE), BF16),
             vmem((PIECES, 16, length), BF16),
             vmem((PIECES, 16, length), BF16),
-            vmem((PIECES, 16, HALF), BF16),
-            vmem((PIECES, 16, HALF), BF16),
-            vmem((PIECES, 16, HALF), BF16),
-            vmem((PIECES, 16, HALF), BF16),
+            vmem((2, PIECES, 16, SIDE), BF16),
+            vmem((2, PIECES, 16, SIDE), BF16),
+            vmem((2, PIECES, 16, SIDE), BF16),
+            vmem((2, PIECES, 16, SIDE), BF16),
             vmem((2, PIECES, 16, HALF), BF16),
             vmem((2, PIECES, 16, HALF), BF16),
             vmem((channels * GROUPS + 16, length), BF16),
             vmem(shape, F32),
             vmem(shape, F32),
             vmem((2 * rows, SIDE), F32),
-            vmem((rows, SIDE), F32),
+            vmem((SIDE * BATCH, SIDE), F32),
             vmem((OWNED // BATCH, 2 * SIDE * BATCH, 2 * SIDE), F32),
-            vmem((rows, SIDE), F32),
+            vmem((SIDE * BATCH, SIDE), F32),
             vmem((rows, SIDE), F32),
             vmem((channels + 16, 2 * length), BF16),
             vmem((2, 16, 64, HALF), F32),
@@ -622,8 +622,8 @@
             vmem((3, 64, HALF), BF16),
             dma((12,)),
         ]
-        + [dma] * 6
-        + [dma((2,))] * 2
+        + [dma] * 2
+        + [dma((2,))] * 6
         + [dma, dma((GROUPS, len(CHUNKS))), dma, dma]
         + [dma((3,))] * 4,
         compiler_params=pltpu.CompilerParams(

time: 73.3 us -> 72 us (0.982); the launches traced: 73.1 us -> 71.1 us
  Pallas kernels: 72.5 us -> 70.4 us
    pallas_call x1, Pallas kernels: 70.2 us -> 68.1 us  [per_device(): pl.pallas_call(whole_kernel, out_shape=(jax.ShapeDtypeStruct(shape, BF16)...]
where the time goes in v6:
time: 72 us; the launch traced here: 71.1 us
  Pallas kernels  70.4 us (98%)
    pallas_call x1, Pallas kernels, per_device(): pl.pallas_call(whole_kernel, out_shape=(jax.ShapeDtypeStruct(shape, BF16)...  68.1 us
    pallas_call x1, Pallas kernels, per_device(): pl.pallas_call(settle_kernel, out_shape=tuple((jax.ShapeDtypeStruct(r.sha...  2.3 us

profile of v6, /device:TPU:16, one launch (start us, length us, event | category | flops | bytes accessed | tf_op | source)
XLA Modules:
  0.0 71.1 jit_solution(12028624333232145647)
XLA Ops:
  0.6 68.1 %shard_map.155 = (bf16[240,512]{1,0:T(8,128)(2,1)}, bf16[240,512]{1,0:T(8,128)(2,1)}, bf16[240,512]{1,0:T(8,128)(2,1)}, f32[240,512]{1,0:T(8,128)}, f32[60,240]{1,0:T(8,128)}) custom-call(bf16[240,512]{1,0:T(8,128)(2,1)} %gate_hbm.1, bf16[240,512]{1,0:T(8,128)(2,1)} %key_hbm.1, bf16[240,512]{1,0:T(8,128)(2,1)} %value_hbm.1, f32[240,512]{1,0:T(8,128)} %filt_hbm.1, ...), custom_call_target="tpu_custom_call" | custom-call | tf_op jit(solution)/shard_map/pallas_call | solution.py:567
  68.8 2.3 %shard_map.156 = (bf16[240,512]{1,0:T(8,128)(2,1)}, bf16[240,512]{1,0:T(8,128)(2,1)}, bf16[240,512]{1,0:T(8,128)(2,1)}, f32[240,512]{1,0:T(8,128)}, f32[60,240]{1,0:T(8,128)}) custom-call(bf16[240,512]{1,0:T(8,128)(2,1)} %get-tuple-element.15.refs_0_, bf16[240,512]{1,0:T(8,128)(2,1)} %get-tuple-element.16.refs_1_, ...), custom_call_target="tpu_custom_call" | custom-call | tf_op jit(solution)/shard_map/pallas_call | solution.py:633

commit v7 on v6

--- a/solution.py
+++ b/solution.py
@@ -23,7 +23,7 @@
 CHUNKS = ((0, 48), (48, 32), (80, 48), (128, 32), (160, 48), (208, 32))
 FLIGHT = 3
 A1POS = 2
-OWNPOS = 2
+OWNPOS = 1
 MESH = pl.DeviceIdType.MESH
 
 

time: 72 us -> 72 us (level)
  no operation moved by 1% of the time
where the time goes in v7:
time: 72 us; the launch traced here: 71 us
  Pallas kernels  70.4 us (98%)
    pallas_call x1, Pallas kernels, per_device(): pl.pallas_call(whole_kernel, out_shape=(jax.ShapeDtypeStruct(shape, BF16)...  68.1 us
    pallas_call x1, Pallas kernels, per_device(): pl.pallas_call(settle_kernel, out_shape=tuple((jax.ShapeDtypeStruct(r.sha...  2.3 us

profile of v7, /device:TPU:16, one launch (start us, length us, event | category | flops | bytes accessed | tf_op | source)
XLA Modules:
  0.0 71.0 jit_solution(9982607023662371242)
XLA Ops:
  0.6 68.1 %shard_map.155 = (bf16[240,512]{1,0:T(8,128)(2,1)}, bf16[240,512]{1,0:T(8,128)(2,1)}, bf16[240,512]{1,0:T(8,128)(2,1)}, f32[240,512]{1,0:T(8,128)}, f32[60,240]{1,0:T(8,128)}) custom-call(bf16[240,512]{1,0:T(8,128)(2,1)} %gate_hbm.1, bf16[240,512]{1,0:T(8,128)(2,1)} %key_hbm.1, bf16[240,512]{1,0:T(8,128)(2,1)} %value_hbm.1, f32[240,512]{1,0:T(8,128)} %filt_hbm.1, ...), custom_call_target="tpu_custom_call" | custom-call | tf_op jit(solution)/shard_map/pallas_call | solution.py:567
  68.7 2.3 %shard_map.156 = (bf16[240,512]{1,0:T(8,128)(2,1)}, bf16[240,512]{1,0:T(8,128)(2,1)}, bf16[240,512]{1,0:T(8,128)(2,1)}, f32[240,512]{1,0:T(8,128)}, f32[60,240]{1,0:T(8,128)}) custom-call(bf16[240,512]{1,0:T(8,128)(2,1)} %get-tuple-element.15.refs_0_, bf16[240,512]{1,0:T(8,128)(2,1)} %get-tuple-element.16.refs_1_, ...), custom_call_target="tpu_custom_call" | custom-call | tf_op jit(solution)/shard_map/pallas_call | solution.py:633
